TPU v7x, 1024 devices: a whole 4x4x32 slice. The times are simulated.
1024 devices in a mesh: dp: 32 (over x, z_hi, y), mp: 32 (over z_lo, core).
Axes of the slice: x: 4, y: 4, z: 32 (z_hi: 2, z_lo: 16; z = z_hi * 16 + z_lo), core: 2. Of those that a mesh axis runs over, the one named last changes fastest.
Arguments:
- image_emb: float32 [4096, 1152], P('dp', 'mp'), may hold values from -0.8 to 0.8
- text_emb: float32 [4096, 1152], P('dp', 'mp'), may hold values from -0.8 to 0.8
- log_scale: float32 [1], replicated, may hold values from 0 to 1
- logit_bias: float32 [1], replicated, may hold values from -6 to -4
Outputs:
- grad_image: float32 [4096, 1152], P('dp', 'mp')
- grad_text: float32 [4096, 1152], P('dp', 'mp')
All inputs are finite; a program needn't handle non-finite values.
Results may differ from a plain program's by a relative error of at most 0.00007.
Values sent between devices are 32-bit elements; how exact they have to be, the bound alone decides.
No kernel may reach another device: no remote copies, remote signals or barrier semaphores. Data moves between devices by JAX's collectives and lax.ppermute only.
A program may use at most 32 MiB of HBM per device.

v0:
```python
import jax
import jax.numpy as jnp
from jax import lax
from jax.sharding import PartitionSpec as P


def shifted(value, axis, steps):
    count = lax.axis_size(axis)
    pairs = [(source, (source + steps) % count) for source in range(count)]
    return lax.ppermute(value, axis, pairs)


def record(k, block, partial_all, seen, image_emb):
    group = block.shape[0]
    part = jnp.dot(
        image_emb, block.T, preferred_element_type=jnp.float32, precision=lax.Precision.HIGHEST
    )
    zero = jnp.zeros((), jnp.int32)
    place = (k * group).astype(jnp.int32)
    partial_all = lax.dynamic_update_slice(partial_all, part, (zero, place))
    seen = lax.dynamic_update_slice(seen, block, (place, zero))
    return (partial_all, seen)


def coefficients(summed, scale, bias):
    logits = scale * summed + bias
    row_ids = lax.broadcasted_iota(jnp.int32, logits.shape, 0)
    col_ids = lax.broadcasted_iota(jnp.int32, logits.shape, 1)
    label = jnp.where(row_ids == col_ids, 1.0, -1.0).astype(jnp.float32)
    return -label * jax.nn.sigmoid(-label * logits)


def on_device(image_emb, text_emb, log_scale, logit_bias):
    scale = jnp.exp(log_scale[0])
    bias = logit_bias[0]
    cycle = lax.axis_size("dp")
    me = lax.axis_index("dp")
    group = image_emb.shape[0]
    narrow = image_emb.shape[1]
    partial_all = jnp.zeros((group, cycle * group), jnp.float32)
    seen = jnp.zeros((cycle * group, narrow), jnp.float32)

    def step(k, carry):
        block, partial_all, seen = carry
        partial_all, seen = record(k, block, partial_all, seen, image_emb)
        block = shifted(block, "dp", 1)
        return (block, partial_all, seen)

    block, partial_all, seen = lax.fori_loop(0, cycle - 1, step, (text_emb, partial_all, seen))
    partial_all, seen = record(
        jnp.asarray(cycle - 1, jnp.int32), block, partial_all, seen, image_emb
    )
    summed = lax.psum(partial_all, "mp")
    coef_all = coefficients(summed, scale, bias)
    grad_image = scale * jnp.dot(
        coef_all, seen, preferred_element_type=jnp.float32, precision=lax.Precision.HIGHEST
    )
    terms = scale * jnp.dot(
        coef_all.T, image_emb, preferred_element_type=jnp.float32, precision=lax.Precision.HIGHEST
    )
    terms = terms.reshape(cycle, group, narrow)
    source = jnp.mod(me - jnp.arange(cycle, dtype=jnp.int32), cycle)
    ordered = jnp.take(terms, source, axis=0)
    returned = lax.all_to_all(ordered, "dp", split_axis=0, concat_axis=0, tiled=True)
    grad_text = jnp.sum(returned, axis=0)
    return (grad_image, grad_text)


def solution(mesh):
    return jax.shard_map(
        on_device,
        mesh=mesh,
        in_specs=(P("dp", "mp"), P("dp", "mp"), P(), P()),
        out_specs=(P("dp", "mp"), P("dp", "mp")),
        check_vma=False,
    )
```

profile of v0, /device:TPU:8, one launch (start us, length us, event | category | flops | bytes accessed | tf_op | source)
XLA Modules:
  0.0 1636.5 jit_solution(10792617056555395412)
XLA Ops:
  7.9 864.9 %while.17 = (s32[]{:T(128)}, f32[128,36]{0,1:T(8,128)S(1)}, f32[128,4096]{1,0:T(8,128)S(1)}, f32[4096,36]{0,1:T(8,128)S(1)}, f32[128,36]{0,1:T(8,128)S(1)}, /*index=5*/s32[]{:T(128)}, s32[]{:T(128)}, s32[]{:T(128)}, s32[]{:T(128)}) while((s32[]{:T(128)}, f32[128,36]{0,1:T(8,128)S(1)}, f32[128,4096]{1,0:T(8,128)S(1)}, ...), condition=%wide.region_1.0_spmd, body=%wide.region_0.0_spmd.sunk | while | flops 7077894 | bytes 258235 | solution.py:49
  7.9 3.5 collective-permute-start
  11.7 12.9 collective-permute-done
  24.7 1.9 collective-permute-start
  26.9 26.0 %collective-permute-done = f32[128,36]{0,1:T(8,128)S(1)} collective-permute-done((f32[128,36]{0,1:T(8,128)S(1)}, f32[128,36]{0,1:T(8,128)S(1)}, u32[]{:S(2)}, u32[]{:S(2)}) %collective-permute-start) | collective-permute-done | bytes 18464 | tf_op jit(solution)/shard_map/while/body/eval_jaxpr/ppermute | solution.py:10
  52.9 1.9 collective-permute-start
  55.1 26.0 %collective-permute-done = f32[128,36]{0,1:T(8,128)S(1)} collective-permute-done((f32[128,36]{0,1:T(8,128)S(1)}, f32[128,36]{0,1:T(8,128)S(1)}, u32[]{:S(2)}, u32[]{:S(2)}) %collective-permute-start) | collective-permute-done | bytes 18464 | tf_op jit(solution)/shard_map/while/body/eval_jaxpr/ppermute | solution.py:10
  81.1 1.9 collective-permute-start
  83.3 26.1 %collective-permute-done = f32[128,36]{0,1:T(8,128)S(1)} collective-permute-done((f32[128,36]{0,1:T(8,128)S(1)}, f32[128,36]{0,1:T(8,128)S(1)}, u32[]{:S(2)}, u32[]{:S(2)}) %collective-permute-start) | collective-permute-done | bytes 18464 | tf_op jit(solution)/shard_map/while/body/eval_jaxpr/ppermute | solution.py:10
  111.6 26.0 %collective-permute-done = f32[128,36]{0,1:T(8,128)S(1)} collective-permute-done((f32[128,36]{0,1:T(8,128)S(1)}, f32[128,36]{0,1:T(8,128)S(1)}, u32[]{:S(2)}, u32[]{:S(2)}) %collective-permute-start) | collective-permute-done | bytes 18464 | tf_op jit(solution)/shard_map/while/body/eval_jaxpr/ppermute | solution.py:10
  139.9 26.0 %collective-permute-done = f32[128,36]{0,1:T(8,128)S(1)} collective-permute-done((f32[128,36]{0,1:T(8,128)S(1)}, f32[128,36]{0,1:T(8,128)S(1)}, u32[]{:S(2)}, u32[]{:S(2)}) %collective-permute-start) | collective-permute-done | bytes 18464 | tf_op jit(solution)/shard_map/while/body/eval_jaxpr/ppermute | solution.py:10
  168.1 26.0 %collective-permute-done = f32[128,36]{0,1:T(8,128)S(1)} collective-permute-done((f32[128,36]{0,1:T(8,128)S(1)}, f32[128,36]{0,1:T(8,128)S(1)}, u32[]{:S(2)}, u32[]{:S(2)}) %collective-permute-start) | collective-permute-done | bytes 18464 | tf_op jit(solution)/shard_map/while/body/eval_jaxpr/ppermute | solution.py:10
  196.3 26.0 %collective-permute-done = f32[128,36]{0,1:T(8,128)S(1)} collective-permute-done((f32[128,36]{0,1:T(8,128)S(1)}, f32[128,36]{0,1:T(8,128)S(1)}, u32[]{:S(2)}, u32[]{:S(2)}) %collective-permute-start) | collective-permute-done | bytes 18464 | tf_op jit(solution)/shard_map/while/body/eval_jaxpr/ppermute | solution.py:10
  224.5 26.0 %collective-permute-done = f32[128,36]{0,1:T(8,128)S(1)} collective-permute-done((f32[128,36]{0,1:T(8,128)S(1)}, f32[128,36]{0,1:T(8,128)S(1)}, u32[]{:S(2)}, u32[]{:S(2)}) %collective-permute-start) | collective-permute-done | bytes 18464 | tf_op jit(solution)/shard_map/while/body/eval_jaxpr/ppermute | solution.py:10
  252.7 26.0 %collective-permute-done = f32[128,36]{0,1:T(8,128)S(1)} collective-permute-done((f32[128,36]{0,1:T(8,128)S(1)}, f32[128,36]{0,1:T(8,128)S(1)}, u32[]{:S(2)}, u32[]{:S(2)}) %collective-permute-start) | collective-permute-done | bytes 18464 | tf_op jit(solution)/shard_map/while/body/eval_jaxpr/ppermute | solution.py:10
  278.7 1.9 collective-permute-start
  280.9 26.0 %collective-permute-done = f32[128,36]{0,1:T(8,128)S(1)} collective-permute-done((f32[128,36]{0,1:T(8,128)S(1)}, f32[128,36]{0,1:T(8,128)S(1)}, u32[]{:S(2)}, u32[]{:S(2)}) %collective-permute-start) | collective-permute-done | bytes 18464 | tf_op jit(solution)/shard_map/while/body/eval_jaxpr/ppermute | solution.py:10
  306.9 1.9 collective-permute-start
  309.2 26.0 %collective-permute-done = f32[128,36]{0,1:T(8,128)S(1)} collective-permute-done((f32[128,36]{0,1:T(8,128)S(1)}, f32[128,36]{0,1:T(8,128)S(1)}, u32[]{:S(2)}, u32[]{:S(2)}) %collective-permute-start) | collective-permute-done | bytes 18464 | tf_op jit(solution)/shard_map/while/body/eval_jaxpr/ppermute | solution.py:10
  337.4 26.0 %collective-permute-done = f32[128,36]{0,1:T(8,128)S(1)} collective-permute-done((f32[128,36]{0,1:T(8,128)S(1)}, f32[128,36]{0,1:T(8,128)S(1)}, u32[]{:S(2)}, u32[]{:S(2)}) %collective-permute-start) | collective-permute-done | bytes 18464 | tf_op jit(solution)/shard_map/while/body/eval_jaxpr/ppermute | solution.py:10
  365.6 26.0 %collective-permute-done = f32[128,36]{0,1:T(8,128)S(1)} collective-permute-done((f32[128,36]{0,1:T(8,128)S(1)}, f32[128,36]{0,1:T(8,128)S(1)}, u32[]{:S(2)}, u32[]{:S(2)}) %collective-permute-start) | collective-permute-done | bytes 18464 | tf_op jit(solution)/shard_map/while/body/eval_jaxpr/ppermute | solution.py:10
  393.8 26.0 %collective-permute-done = f32[128,36]{0,1:T(8,128)S(1)} collective-permute-done((f32[128,36]{0,1:T(8,128)S(1)}, f32[128,36]{0,1:T(8,128)S(1)}, u32[]{:S(2)}, u32[]{:S(2)}) %collective-permute-start) | collective-permute-done | bytes 18464 | tf_op jit(solution)/shard_map/while/body/eval_jaxpr/ppermute | solution.py:10
  419.8 1.9 collective-permute-start
  422.0 26.0 %collective-permute-done = f32[128,36]{0,1:T(8,128)S(1)} collective-permute-done((f32[128,36]{0,1:T(8,128)S(1)}, f32[128,36]{0,1:T(8,128)S(1)}, u32[]{:S(2)}, u32[]{:S(2)}) %collective-permute-start) | collective-permute-done | bytes 18464 | tf_op jit(solution)/shard_map/while/body/eval_jaxpr/ppermute | solution.py:10
  450.2 26.0 %collective-permute-done = f32[128,36]{0,1:T(8,128)S(1)} collective-permute-done((f32[128,36]{0,1:T(8,128)S(1)}, f32[128,36]{0,1:T(8,128)S(1)}, u32[]{:S(2)}, u32[]{:S(2)}) %collective-permute-start) | collective-permute-done | bytes 18464 | tf_op jit(solution)/shard_map/while/body/eval_jaxpr/ppermute | solution.py:10
  478.5 26.1 %collective-permute-done = f32[128,36]{0,1:T(8,128)S(1)} collective-permute-done((f32[128,36]{0,1:T(8,128)S(1)}, f32[128,36]{0,1:T(8,128)S(1)}, u32[]{:S(2)}, u32[]{:S(2)}) %collective-permute-start) | collective-permute-done | bytes 18464 | tf_op jit(solution)/shard_map/while/body/eval_jaxpr/ppermute | solution.py:10
  506.8 26.1 %collective-permute-done = f32[128,36]{0,1:T(8,128)S(1)} collective-permute-done((f32[128,36]{0,1:T(8,128)S(1)}, f32[128,36]{0,1:T(8,128)S(1)}, u32[]{:S(2)}, u32[]{:S(2)}) %collective-permute-start) | collective-permute-done | bytes 18464 | tf_op jit(solution)/shard_map/while/body/eval_jaxpr/ppermute | solution.py:10
  532.8 1.9 collective-permute-start
  535.1 26.5 %collective-permute-done = f32[128,36]{0,1:T(8,128)S(1)} collective-permute-done((f32[128,36]{0,1:T(8,128)S(1)}, f32[128,36]{0,1:T(8,128)S(1)}, u32[]{:S(2)}, u32[]{:S(2)}) %collective-permute-start) | collective-permute-done | bytes 18464 | tf_op jit(solution)/shard_map/while/body/eval_jaxpr/ppermute | solution.py:10
  563.8 26.4 %collective-permute-done = f32[128,36]{0,1:T(8,128)S(1)} collective-permute-done((f32[128,36]{0,1:T(8,128)S(1)}, f32[128,36]{0,1:T(8,128)S(1)}, u32[]{:S(2)}, u32[]{:S(2)}) %collective-permute-start) | collective-permute-done | bytes 18464 | tf_op jit(solution)/shard_map/while/body/eval_jaxpr/ppermute | solution.py:10
  590.2 1.9 collective-permute-start
  592.5 26.0 %collective-permute-done = f32[128,36]{0,1:T(8,128)S(1)} collective-permute-done((f32[128,36]{0,1:T(8,128)S(1)}, f32[128,36]{0,1:T(8,128)S(1)}, u32[]{:S(2)}, u32[]{:S(2)}) %collective-permute-start) | collective-permute-done | bytes 18464 | tf_op jit(solution)/shard_map/while/body/eval_jaxpr/ppermute | solution.py:10
  618.5 1.9 collective-permute-start
  620.7 26.0 %collective-permute-done = f32[128,36]{0,1:T(8,128)S(1)} collective-permute-done((f32[128,36]{0,1:T(8,128)S(1)}, f32[128,36]{0,1:T(8,128)S(1)}, u32[]{:S(2)}, u32[]{:S(2)}) %collective-permute-start) | collective-permute-done | bytes 18464 | tf_op jit(solution)/shard_map/while/body/eval_jaxpr/ppermute | solution.py:10
  648.9 26.0 %collective-permute-done = f32[128,36]{0,1:T(8,128)S(1)} collective-permute-done((f32[128,36]{0,1:T(8,128)S(1)}, f32[128,36]{0,1:T(8,128)S(1)}, u32[]{:S(2)}, u32[]{:S(2)}) %collective-permute-start) | collective-permute-done | bytes 18464 | tf_op jit(solution)/shard_map/while/body/eval_jaxpr/ppermute | solution.py:10
  677.1 26.0 %collective-permute-done = f32[128,36]{0,1:T(8,128)S(1)} collective-permute-done((f32[128,36]{0,1:T(8,128)S(1)}, f32[128,36]{0,1:T(8,128)S(1)}, u32[]{:S(2)}, u32[]{:S(2)}) %collective-permute-start) | collective-permute-done | bytes 18464 | tf_op jit(solution)/shard_map/while/body/eval_jaxpr/ppermute | solution.py:10
  705.3 26.4 %collective-permute-done = f32[128,36]{0,1:T(8,128)S(1)} collective-permute-done((f32[128,36]{0,1:T(8,128)S(1)}, f32[128,36]{0,1:T(8,128)S(1)}, u32[]{:S(2)}, u32[]{:S(2)}) %collective-permute-start) | collective-permute-done | bytes 18464 | tf_op jit(solution)/shard_map/while/body/eval_jaxpr/ppermute | solution.py:10
  734.0 26.0 %collective-permute-done = f32[128,36]{0,1:T(8,128)S(1)} collective-permute-done((f32[128,36]{0,1:T(8,128)S(1)}, f32[128,36]{0,1:T(8,128)S(1)}, u32[]{:S(2)}, u32[]{:S(2)}) %collective-permute-start) | collective-permute-done | bytes 18464 | tf_op jit(solution)/shard_map/while/body/eval_jaxpr/ppermute | solution.py:10
  762.2 26.0 %collective-permute-done = f32[128,36]{0,1:T(8,128)S(1)} collective-permute-done((f32[128,36]{0,1:T(8,128)S(1)}, f32[128,36]{0,1:T(8,128)S(1)}, u32[]{:S(2)}, u32[]{:S(2)}) %collective-permute-start) | collective-permute-done | bytes 18464 | tf_op jit(solution)/shard_map/while/body/eval_jaxpr/ppermute | solution.py:10
  790.4 26.0 %collective-permute-done = f32[128,36]{0,1:T(8,128)S(1)} collective-permute-done((f32[128,36]{0,1:T(8,128)S(1)}, f32[128,36]{0,1:T(8,128)S(1)}, u32[]{:S(2)}, u32[]{:S(2)}) %collective-permute-start) | collective-permute-done | bytes 18464 | tf_op jit(solution)/shard_map/while/body/eval_jaxpr/ppermute | solution.py:10
  816.4 1.9 collective-permute-start
  818.6 26.0 %collective-permute-done = f32[128,36]{0,1:T(8,128)S(1)} collective-permute-done((f32[128,36]{0,1:T(8,128)S(1)}, f32[128,36]{0,1:T(8,128)S(1)}, u32[]{:S(2)}, u32[]{:S(2)}) %collective-permute-start) | collective-permute-done | bytes 18464 | tf_op jit(solution)/shard_map/while/body/eval_jaxpr/ppermute | solution.py:10
  846.9 26.0 %collective-permute-done = f32[128,36]{0,1:T(8,128)S(1)} collective-permute-done((f32[128,36]{0,1:T(8,128)S(1)}, f32[128,36]{0,1:T(8,128)S(1)}, u32[]{:S(2)}, u32[]{:S(2)}) %collective-permute-start) | collective-permute-done | bytes 18464 | tf_op jit(solution)/shard_map/while/body/eval_jaxpr/ppermute | solution.py:10
  875.9 689.5 %all-reduce.2.cloned.1.call-done = f32[128,4096]{1,0:T(8,128)} async-done(((f32[128,4096]{1,0:T(8,128)}), f32[128,4096]{1,0:T(8,128)}) %all-reduce.2.cloned.1.call-update) | async-done | bytes 2097168 | tf_op jit(solution)/shard_map/psum | solution.py:53
  1565.4 3.3 convolution_multiply_fusion
  1570.8 29.9 %all-to-all-start = ((f32[32,128,36]{1,2,0:T(8,128)}), f32[32,128,36]{1,2,0:T(8,128)S(1)}, u32[]{:S(2)}, u32[]{:S(2)}) async-start(f32[32,128,36]{1,2,0:T(8,128)} %broadcast_select_fusion), calls=%async_computation | async-start | bytes 1310720 | tf_op jit(solution)/shard_map/all_to_all | solution.py:64
  1600.7 4.6 convolution_multiply_fusion.1
  1605.3 23.6 %all-to-all-done = f32[32,128,36]{1,2,0:T(8,128)S(1)} async-done(((f32[32,128,36]{1,2,0:T(8,128)}), f32[32,128,36]{1,2,0:T(8,128)S(1)}, u32[]{:S(2)}, u32[]{:S(2)}) %all-to-all-start) | async-done | bytes 589856 | tf_op jit(solution)/shard_map/all_to_all | solution.py:64
  (136 shorter events, 52.7 us)
Async XLA Ops:
  7.2 0.7 copy-start.2
  7.2 0.7 copy-start.1
  7.2 1558.2 %all-reduce.2.cloned.1.call-start = ((), (), s32[]{:S(2)}) async-start(), calls=%async_computation.1 | async-start | bytes 4194304 | tf_op jit(solution)/shard_map/psum | solution.py:53
  7.9 16.7 %collective-permute-start = (f32[128,36]{0,1:T(8,128)S(1)}, f32[128,36]{0,1:T(8,128)S(1)}, u32[]{:S(2)}, u32[]{:S(2)}) collective-permute-start(f32[128,36]{0,1:T(8,128)S(1)} %copy.17), channel_id=1, source_target_pairs={{0,32},{32,64},{64,96},{96,128},{128,160},{160,192},{192,224},{224... | collective-permute-start | bytes 55304 | tf_op jit(solution)/shard_map/while/body/eval_jaxpr/ppermute | solution.py:10
  24.7 28.2 %collective-permute-start = (f32[128,36]{0,1:T(8,128)S(1)}, f32[128,36]{0,1:T(8,128)S(1)}, u32[]{:S(2)}, u32[]{:S(2)}) collective-permute-start(f32[128,36]{0,1:T(8,128)S(1)} %copy.17), channel_id=1, source_target_pairs={{0,32},{32,64},{64,96},{96,128},{128,160},{160,192},{192,224},{224... | collective-permute-start | bytes 55304 | tf_op jit(solution)/shard_map/while/body/eval_jaxpr/ppermute | solution.py:10
  52.9 28.2 %collective-permute-start = (f32[128,36]{0,1:T(8,128)S(1)}, f32[128,36]{0,1:T(8,128)S(1)}, u32[]{:S(2)}, u32[]{:S(2)}) collective-permute-start(f32[128,36]{0,1:T(8,128)S(1)} %copy.17), channel_id=1, source_target_pairs={{0,32},{32,64},{64,96},{96,128},{128,160},{160,192},{192,224},{224... | collective-permute-start | bytes 55304 | tf_op jit(solution)/shard_map/while/body/eval_jaxpr/ppermute | solution.py:10
  81.1 28.3 %collective-permute-start = (f32[128,36]{0,1:T(8,128)S(1)}, f32[128,36]{0,1:T(8,128)S(1)}, u32[]{:S(2)}, u32[]{:S(2)}) collective-permute-start(f32[128,36]{0,1:T(8,128)S(1)} %copy.17), channel_id=1, source_target_pairs={{0,32},{32,64},{64,96},{96,128},{128,160},{160,192},{192,224},{224... | collective-permute-start | bytes 55304 | tf_op jit(solution)/shard_map/while/body/eval_jaxpr/ppermute | solution.py:10
  109.4 28.2 %collective-permute-start = (f32[128,36]{0,1:T(8,128)S(1)}, f32[128,36]{0,1:T(8,128)S(1)}, u32[]{:S(2)}, u32[]{:S(2)}) collective-permute-start(f32[128,36]{0,1:T(8,128)S(1)} %copy.17), channel_id=1, source_target_pairs={{0,32},{32,64},{64,96},{96,128},{128,160},{160,192},{192,224},{224... | collective-permute-start | bytes 55304 | tf_op jit(solution)/shard_map/while/body/eval_jaxpr/ppermute | solution.py:10
  137.6 28.2 %collective-permute-start = (f32[128,36]{0,1:T(8,128)S(1)}, f32[128,36]{0,1:T(8,128)S(1)}, u32[]{:S(2)}, u32[]{:S(2)}) collective-permute-start(f32[128,36]{0,1:T(8,128)S(1)} %copy.17), channel_id=1, source_target_pairs={{0,32},{32,64},{64,96},{96,128},{128,160},{160,192},{192,224},{224... | collective-permute-start | bytes 55304 | tf_op jit(solution)/shard_map/while/body/eval_jaxpr/ppermute | solution.py:10
  165.8 28.2 %collective-permute-start = (f32[128,36]{0,1:T(8,128)S(1)}, f32[128,36]{0,1:T(8,128)S(1)}, u32[]{:S(2)}, u32[]{:S(2)}) collective-permute-start(f32[128,36]{0,1:T(8,128)S(1)} %copy.17), channel_id=1, source_target_pairs={{0,32},{32,64},{64,96},{96,128},{128,160},{160,192},{192,224},{224... | collective-permute-start | bytes 55304 | tf_op jit(solution)/shard_map/while/body/eval_jaxpr/ppermute | solution.py:10
  194.1 28.2 %collective-permute-start = (f32[128,36]{0,1:T(8,128)S(1)}, f32[128,36]{0,1:T(8,128)S(1)}, u32[]{:S(2)}, u32[]{:S(2)}) collective-permute-start(f32[128,36]{0,1:T(8,128)S(1)} %copy.17), channel_id=1, source_target_pairs={{0,32},{32,64},{64,96},{96,128},{128,160},{160,192},{192,224},{224... | collective-permute-start | bytes 55304 | tf_op jit(solution)/shard_map/while/body/eval_jaxpr/ppermute | solution.py:10
  222.3 28.2 %collective-permute-start = (f32[128,36]{0,1:T(8,128)S(1)}, f32[128,36]{0,1:T(8,128)S(1)}, u32[]{:S(2)}, u32[]{:S(2)}) collective-permute-start(f32[128,36]{0,1:T(8,128)S(1)} %copy.17), channel_id=1, source_target_pairs={{0,32},{32,64},{64,96},{96,128},{128,160},{160,192},{192,224},{224... | collective-permute-start | bytes 55304 | tf_op jit(solution)/shard_map/while/body/eval_jaxpr/ppermute | solution.py:10
  250.5 28.2 %collective-permute-start = (f32[128,36]{0,1:T(8,128)S(1)}, f32[128,36]{0,1:T(8,128)S(1)}, u32[]{:S(2)}, u32[]{:S(2)}) collective-permute-start(f32[128,36]{0,1:T(8,128)S(1)} %copy.17), channel_id=1, source_target_pairs={{0,32},{32,64},{64,96},{96,128},{128,160},{160,192},{192,224},{224... | collective-permute-start | bytes 55304 | tf_op jit(solution)/shard_map/while/body/eval_jaxpr/ppermute | solution.py:10
  278.7 28.2 %collective-permute-start = (f32[128,36]{0,1:T(8,128)S(1)}, f32[128,36]{0,1:T(8,128)S(1)}, u32[]{:S(2)}, u32[]{:S(2)}) collective-permute-start(f32[128,36]{0,1:T(8,128)S(1)} %copy.17), channel_id=1, source_target_pairs={{0,32},{32,64},{64,96},{96,128},{128,160},{160,192},{192,224},{224... | collective-permute-start | bytes 55304 | tf_op jit(solution)/shard_map/while/body/eval_jaxpr/ppermute | solution.py:10
  306.9 28.2 %collective-permute-start = (f32[128,36]{0,1:T(8,128)S(1)}, f32[128,36]{0,1:T(8,128)S(1)}, u32[]{:S(2)}, u32[]{:S(2)}) collective-permute-start(f32[128,36]{0,1:T(8,128)S(1)} %copy.17), channel_id=1, source_target_pairs={{0,32},{32,64},{64,96},{96,128},{128,160},{160,192},{192,224},{224... | collective-permute-start | bytes 55304 | tf_op jit(solution)/shard_map/while/body/eval_jaxpr/ppermute | solution.py:10
  335.1 28.2 %collective-permute-start = (f32[128,36]{0,1:T(8,128)S(1)}, f32[128,36]{0,1:T(8,128)S(1)}, u32[]{:S(2)}, u32[]{:S(2)}) collective-permute-start(f32[128,36]{0,1:T(8,128)S(1)} %copy.17), channel_id=1, source_target_pairs={{0,32},{32,64},{64,96},{96,128},{128,160},{160,192},{192,224},{224... | collective-permute-start | bytes 55304 | tf_op jit(solution)/shard_map/while/body/eval_jaxpr/ppermute | solution.py:10
  363.3 28.2 %collective-permute-start = (f32[128,36]{0,1:T(8,128)S(1)}, f32[128,36]{0,1:T(8,128)S(1)}, u32[]{:S(2)}, u32[]{:S(2)}) collective-permute-start(f32[128,36]{0,1:T(8,128)S(1)} %copy.17), channel_id=1, source_target_pairs={{0,32},{32,64},{64,96},{96,128},{128,160},{160,192},{192,224},{224... | collective-permute-start | bytes 55304 | tf_op jit(solution)/shard_map/while/body/eval_jaxpr/ppermute | solution.py:10
  391.6 28.2 %collective-permute-start = (f32[128,36]{0,1:T(8,128)S(1)}, f32[128,36]{0,1:T(8,128)S(1)}, u32[]{:S(2)}, u32[]{:S(2)}) collective-permute-start(f32[128,36]{0,1:T(8,128)S(1)} %copy.17), channel_id=1, source_target_pairs={{0,32},{32,64},{64,96},{96,128},{128,160},{160,192},{192,224},{224... | collective-permute-start | bytes 55304 | tf_op jit(solution)/shard_map/while/body/eval_jaxpr/ppermute | solution.py:10
  419.8 28.2 %collective-permute-start = (f32[128,36]{0,1:T(8,128)S(1)}, f32[128,36]{0,1:T(8,128)S(1)}, u32[]{:S(2)}, u32[]{:S(2)}) collective-permute-start(f32[128,36]{0,1:T(8,128)S(1)} %copy.17), channel_id=1, source_target_pairs={{0,32},{32,64},{64,96},{96,128},{128,160},{160,192},{192,224},{224... | collective-permute-start | bytes 55304 | tf_op jit(solution)/shard_map/while/body/eval_jaxpr/ppermute | solution.py:10
  448.0 28.2 %collective-permute-start = (f32[128,36]{0,1:T(8,128)S(1)}, f32[128,36]{0,1:T(8,128)S(1)}, u32[]{:S(2)}, u32[]{:S(2)}) collective-permute-start(f32[128,36]{0,1:T(8,128)S(1)} %copy.17), channel_id=1, source_target_pairs={{0,32},{32,64},{64,96},{96,128},{128,160},{160,192},{192,224},{224... | collective-permute-start | bytes 55304 | tf_op jit(solution)/shard_map/while/body/eval_jaxpr/ppermute | solution.py:10
  476.2 28.3 %collective-permute-start = (f32[128,36]{0,1:T(8,128)S(1)}, f32[128,36]{0,1:T(8,128)S(1)}, u32[]{:S(2)}, u32[]{:S(2)}) collective-permute-start(f32[128,36]{0,1:T(8,128)S(1)} %copy.17), channel_id=1, source_target_pairs={{0,32},{32,64},{64,96},{96,128},{128,160},{160,192},{192,224},{224... | collective-permute-start | bytes 55304 | tf_op jit(solution)/shard_map/while/body/eval_jaxpr/ppermute | solution.py:10
  504.5 28.3 %collective-permute-start = (f32[128,36]{0,1:T(8,128)S(1)}, f32[128,36]{0,1:T(8,128)S(1)}, u32[]{:S(2)}, u32[]{:S(2)}) collective-permute-start(f32[128,36]{0,1:T(8,128)S(1)} %copy.17), channel_id=1, source_target_pairs={{0,32},{32,64},{64,96},{96,128},{128,160},{160,192},{192,224},{224... | collective-permute-start | bytes 55304 | tf_op jit(solution)/shard_map/while/body/eval_jaxpr/ppermute | solution.py:10
  532.8 28.8 %collective-permute-start = (f32[128,36]{0,1:T(8,128)S(1)}, f32[128,36]{0,1:T(8,128)S(1)}, u32[]{:S(2)}, u32[]{:S(2)}) collective-permute-start(f32[128,36]{0,1:T(8,128)S(1)} %copy.17), channel_id=1, source_target_pairs={{0,32},{32,64},{64,96},{96,128},{128,160},{160,192},{192,224},{224... | collective-permute-start | bytes 55304 | tf_op jit(solution)/shard_map/while/body/eval_jaxpr/ppermute | solution.py:10
  561.6 28.6 %collective-permute-start = (f32[128,36]{0,1:T(8,128)S(1)}, f32[128,36]{0,1:T(8,128)S(1)}, u32[]{:S(2)}, u32[]{:S(2)}) collective-permute-start(f32[128,36]{0,1:T(8,128)S(1)} %copy.17), channel_id=1, source_target_pairs={{0,32},{32,64},{64,96},{96,128},{128,160},{160,192},{192,224},{224... | collective-permute-start | bytes 55304 | tf_op jit(solution)/shard_map/while/body/eval_jaxpr/ppermute | solution.py:10
  590.2 28.2 %collective-permute-start = (f32[128,36]{0,1:T(8,128)S(1)}, f32[128,36]{0,1:T(8,128)S(1)}, u32[]{:S(2)}, u32[]{:S(2)}) collective-permute-start(f32[128,36]{0,1:T(8,128)S(1)} %copy.17), channel_id=1, source_target_pairs={{0,32},{32,64},{64,96},{96,128},{128,160},{160,192},{192,224},{224... | collective-permute-start | bytes 55304 | tf_op jit(solution)/shard_map/while/body/eval_jaxpr/ppermute | solution.py:10
  618.5 28.2 %collective-permute-start = (f32[128,36]{0,1:T(8,128)S(1)}, f32[128,36]{0,1:T(8,128)S(1)}, u32[]{:S(2)}, u32[]{:S(2)}) collective-permute-start(f32[128,36]{0,1:T(8,128)S(1)} %copy.17), channel_id=1, source_target_pairs={{0,32},{32,64},{64,96},{96,128},{128,160},{160,192},{192,224},{224... | collective-permute-start | bytes 55304 | tf_op jit(solution)/shard_map/while/body/eval_jaxpr/ppermute | solution.py:10
  646.7 28.2 %collective-permute-start = (f32[128,36]{0,1:T(8,128)S(1)}, f32[128,36]{0,1:T(8,128)S(1)}, u32[]{:S(2)}, u32[]{:S(2)}) collective-permute-start(f32[128,36]{0,1:T(8,128)S(1)} %copy.17), channel_id=1, source_target_pairs={{0,32},{32,64},{64,96},{96,128},{128,160},{160,192},{192,224},{224... | collective-permute-start | bytes 55304 | tf_op jit(solution)/shard_map/while/body/eval_jaxpr/ppermute | solution.py:10
  674.9 28.2 %collective-permute-start = (f32[128,36]{0,1:T(8,128)S(1)}, f32[128,36]{0,1:T(8,128)S(1)}, u32[]{:S(2)}, u32[]{:S(2)}) collective-permute-start(f32[128,36]{0,1:T(8,128)S(1)} %copy.17), channel_id=1, source_target_pairs={{0,32},{32,64},{64,96},{96,128},{128,160},{160,192},{192,224},{224... | collective-permute-start | bytes 55304 | tf_op jit(solution)/shard_map/while/body/eval_jaxpr/ppermute | solution.py:10
  703.1 28.6 %collective-permute-start = (f32[128,36]{0,1:T(8,128)S(1)}, f32[128,36]{0,1:T(8,128)S(1)}, u32[]{:S(2)}, u32[]{:S(2)}) collective-permute-start(f32[128,36]{0,1:T(8,128)S(1)} %copy.17), channel_id=1, source_target_pairs={{0,32},{32,64},{64,96},{96,128},{128,160},{160,192},{192,224},{224... | collective-permute-start | bytes 55304 | tf_op jit(solution)/shard_map/while/body/eval_jaxpr/ppermute | solution.py:10
  731.8 28.2 %collective-permute-start = (f32[128,36]{0,1:T(8,128)S(1)}, f32[128,36]{0,1:T(8,128)S(1)}, u32[]{:S(2)}, u32[]{:S(2)}) collective-permute-start(f32[128,36]{0,1:T(8,128)S(1)} %copy.17), channel_id=1, source_target_pairs={{0,32},{32,64},{64,96},{96,128},{128,160},{160,192},{192,224},{224... | collective-permute-start | bytes 55304 | tf_op jit(solution)/shard_map/while/body/eval_jaxpr/ppermute | solution.py:10
  760.0 28.2 %collective-permute-start = (f32[128,36]{0,1:T(8,128)S(1)}, f32[128,36]{0,1:T(8,128)S(1)}, u32[]{:S(2)}, u32[]{:S(2)}) collective-permute-start(f32[128,36]{0,1:T(8,128)S(1)} %copy.17), channel_id=1, source_target_pairs={{0,32},{32,64},{64,96},{96,128},{128,160},{160,192},{192,224},{224... | collective-permute-start | bytes 55304 | tf_op jit(solution)/shard_map/while/body/eval_jaxpr/ppermute | solution.py:10
  788.2 28.2 %collective-permute-start = (f32[128,36]{0,1:T(8,128)S(1)}, f32[128,36]{0,1:T(8,128)S(1)}, u32[]{:S(2)}, u32[]{:S(2)}) collective-permute-start(f32[128,36]{0,1:T(8,128)S(1)} %copy.17), channel_id=1, source_target_pairs={{0,32},{32,64},{64,96},{96,128},{128,160},{160,192},{192,224},{224... | collective-permute-start | bytes 55304 | tf_op jit(solution)/shard_map/while/body/eval_jaxpr/ppermute | solution.py:10
  816.4 28.2 %collective-permute-start = (f32[128,36]{0,1:T(8,128)S(1)}, f32[128,36]{0,1:T(8,128)S(1)}, u32[]{:S(2)}, u32[]{:S(2)}) collective-permute-start(f32[128,36]{0,1:T(8,128)S(1)} %copy.17), channel_id=1, source_target_pairs={{0,32},{32,64},{64,96},{96,128},{128,160},{160,192},{192,224},{224... | collective-permute-start | bytes 55304 | tf_op jit(solution)/shard_map/while/body/eval_jaxpr/ppermute | solution.py:10
  844.6 28.2 %collective-permute-start = (f32[128,36]{0,1:T(8,128)S(1)}, f32[128,36]{0,1:T(8,128)S(1)}, u32[]{:S(2)}, u32[]{:S(2)}) collective-permute-start(f32[128,36]{0,1:T(8,128)S(1)} %copy.17), channel_id=1, source_target_pairs={{0,32},{32,64},{64,96},{96,128},{128,160},{160,192},{192,224},{224... | collective-permute-start | bytes 55304 | tf_op jit(solution)/shard_map/while/body/eval_jaxpr/ppermute | solution.py:10
  873.2 1.3 copy-start
  1570.8 58.2 %all-to-all-start = ((f32[32,128,36]{1,2,0:T(8,128)}), f32[32,128,36]{1,2,0:T(8,128)S(1)}, u32[]{:S(2)}, u32[]{:S(2)}) async-start(f32[32,128,36]{1,2,0:T(8,128)} %broadcast_select_fusion), calls=%async_computation | async-start | bytes 1310720 | tf_op jit(solution)/shard_map/all_to_all | solution.py:64
Sparse Core Ops, SparseCore 0:
  874.7 690.6 all-reduce.1
where the time goes:
time: 1640 us
  waiting for transfers between devices  1510 us (92%)
  starting transfers between devices  90.7 us (6%)
  matrix products  17.1 us (1%)
    ppermute x31, waiting for transfers between devices, shifted(): return lax.ppermute(value, axis, pairs)  794 us
    psum x1, waiting for transfers between devices, on_device(): summed = lax.psum(partial_all, 'mp')  689 us
    ppermute x31, starting transfers between devices, shifted(): return lax.ppermute(value, axis, pairs)  60.7 us
  transfers between devices with their start and end apart: 33, of which 33 were waited for; matrix products, arithmetic and copies ran while one was open for 1% of the time, Pallas kernels for 0%

commit v1 on v0

v1 whole, which is shorter than its diff:
```python
import functools

import jax
import jax.numpy as jnp
from jax import lax
from jax.experimental import pallas as pl
from jax.experimental.pallas import tpu as pltpu
from jax.sharding import Mesh, PartitionSpec as P

LANES = 128
VMEM = pl.BlockSpec(memory_space=pltpu.VMEM)
SMEM = pl.BlockSpec(memory_space=pltpu.SMEM)


def rows_first(block):
    narrow, rows = block.shape
    filled = jnp.concatenate([block, jnp.zeros((LANES - narrow, rows), block.dtype)], axis=0)
    return filled.T


def only(block, width):
    lane = lax.broadcasted_iota(jnp.int32, block.shape, 1)
    return jnp.where(lane < width, block, 0.0)


def shift(block, lanes):
    lanes = lanes % LANES
    return block if lanes == 0 else pltpu.roll(block, lanes, 1)


def split_kernel(sizes, image_ref, text_ref, out_ref):
    high, low, of_i, of_j = sizes
    narrow, rows = image_ref.shape
    image, text = rows_first(image_ref[...]), rows_first(text_ref[...])
    group, small = rows // of_i, rows // of_j
    halves = group // small
    near = low // of_i
    images = []
    for i in range(of_i):
        total = None
        for h in range(halves):
            start = i * group + h * small
            part = shift(image[start : start + small], h * narrow)
            total = part if total is None else total + part
        images.append(total)
    texts = [shift(text[j * small : (j + 1) * small], halves * narrow) for j in range(of_j)]
    for zh in range(high):
        for zl in range(low):
            out_ref[zh * low + zl] = images[zl // near] + texts[zh * near + zl % near]


def widen_kernel(sizes, narrow, got_ref, image_ref, text_ref):
    high, low, halves = sizes
    small = got_ref.shape[1]
    copies_i, copies_t = image_ref.shape[0], text_ref.shape[0]
    tiles = -(-low * narrow // LANES)
    for zh in range(high):
        for h in range(halves + 1):
            acc = [None] * tiles
            for zl in range(low):
                part = got_ref[zh * low + zl]
                lane = lax.broadcasted_iota(jnp.int32, part.shape, 1)
                tile, at = divmod(zl * narrow, LANES)
                moved = shift(part, at - h * narrow)
                end = at + narrow
                mine = jnp.where((lane >= at) & (lane < end), moved, 0.0)
                acc[tile] = mine if acc[tile] is None else acc[tile] + mine
                if end > LANES:
                    mine = jnp.where(lane < end - LANES, moved, 0.0)
                    acc[tile + 1] = mine
            for tile in range(tiles):
                lo = tile * LANES
                hi = min(lo + LANES, low * narrow)
                value = acc[tile][:, : hi - lo]
                if h < halves:
                    at = (zh * halves + h) * small
                    for k in range(copies_i):
                        image_ref[k, at : at + small, lo:hi] = value
                else:
                    for k in range(copies_t):
                        text_ref[k, zh * small : (zh + 1) * small, lo:hi] = value


def logits_kernel(image_ref, text_ref, out_ref):
    a, m, w = image_ref.shape
    b, n, _ = text_ref.shape
    out_ref[...] = lax.dot_general(
        image_ref[...].reshape(a * m, w),
        text_ref[...].reshape(b * n, w),
        (((1,), (1,)), ((), ())),
        preferred_element_type=jnp.float32,
        precision=lax.Precision.HIGHEST,
    )


def grads_kernel(sizes, at_ref, log_scale_ref, bias_ref, mine_ref, other_ref, image_ref, text_ref, gi_ref, gt_ref):
    high, halves, small, rows, of_y = sizes
    a, m, w = image_ref.shape
    b, n, _ = text_ref.shape
    scale = jnp.exp(jnp.full((1, 1), log_scale_ref[0], jnp.float32))
    logits = scale * (mine_ref[...] + other_ref[...]) + bias_ref[0]
    x, y, i, j = at_ref[0], at_ref[1], at_ref[2], at_ref[3]
    r = lax.broadcasted_iota(jnp.int32, logits.shape, 0)
    yy, zh, inner = r // m, (r % m) // (halves * small), r % (halves * small)
    row_ids = (x * high * of_y + zh * of_y + yy) * rows + i * (halves * small) + inner
    c = lax.broadcasted_iota(jnp.int32, logits.shape, 1)
    xx, zh, inner = c // n, (c % n) // small, c % small
    col_ids = (xx * high * of_y + zh * of_y + y) * rows + j * small + inner
    label = jnp.where(row_ids == col_ids, 1.0, -1.0)
    coef = -label * jax.nn.sigmoid(-label * logits)
    image = image_ref[...].reshape(a * m, w)
    text = text_ref[...].reshape(b * n, w)
    dot = functools.partial(
        lax.dot_general, preferred_element_type=jnp.float32, precision=lax.Precision.HIGHEST
    )
    gi_ref[...] = (scale * dot(coef, text, (((1,), (0,)), ((), ())))).reshape(a, m, w)
    gt_ref[...] = (scale * dot(coef, image, (((0,), (0,)), ((), ())))).reshape(b, n, w)


def narrow_kernel(sizes, narrow, image_ref, text_ref, out_ref):
    high, low, halves = sizes
    small = out_ref.shape[1]
    tiles = -(-low * narrow // LANES)
    width = low * narrow

    def summed(ref, start):
        found = []
        for tile in range(tiles):
            lo = tile * LANES
            hi = min(lo + LANES, width)
            value = ref[0, start : start + small, lo:hi]
            for k in range(1, ref.shape[0]):
                value = value + ref[k, start : start + small, lo:hi]
            if hi - lo < LANES:
                value = jnp.concatenate([value, jnp.zeros((small, LANES - hi + lo), value.dtype)], axis=1)
            found.append(value)
        return found

    for zh in range(high):
        sums = [summed(image_ref, (zh * halves + h) * small) for h in range(halves)]
        sums.append(summed(text_ref, zh * small))
        for zl in range(low):
            tile, at = divmod(zl * narrow, LANES)
            total = None
            for h, value in enumerate(sums):
                lane = lax.broadcasted_iota(jnp.int32, value[0].shape, 1)
                to = h * narrow
                moved = shift(value[tile], to - at)
                here = min(narrow, LANES - at)
                part = jnp.where((lane >= to) & (lane < to + here), moved, 0.0)
                if here < narrow:
                    moved = shift(value[tile + 1], to - at)
                    part = part + jnp.where((lane >= to + here) & (lane < to + narrow), moved, 0.0)
                total = part if total is None else total + part
            out_ref[zh * low + zl] = total


def collect_kernel(sizes, got_ref, image_ref, text_ref):
    high, low, of_i, of_j = sizes
    narrow, rows = image_ref.shape
    small = got_ref.shape[1]
    group = rows // of_i
    halves = group // small
    near = low // of_i

    def total(sources):
        value = got_ref[sources[0]]
        for source in sources[1:]:
            value = value + got_ref[source]
        return value

    images = []
    for i in range(of_i):
        value = total([zh * low + i * near + k for zh in range(high) for k in range(near)])
        for h in range(halves):
            images.append(shift(value, -h * narrow))
    texts = []
    for j in range(of_j):
        zh, k = divmod(j, near)
        texts.append(shift(total([zh * low + i * near + k for i in range(of_i)]), -halves * narrow))
    image_ref[...] = jnp.concatenate(images, axis=0).T[:narrow]
    text_ref[...] = jnp.concatenate(texts, axis=0).T[:narrow]


def call(kernel, outs, *operands, scalars=0):
    many = isinstance(outs, list)
    shapes = [jax.ShapeDtypeStruct(s, jnp.float32) for s in (outs if many else [outs])]
    return pl.pallas_call(
        kernel,
        out_shape=shapes if many else shapes[0],
        in_specs=[SMEM] * scalars + [VMEM] * (len(operands) - scalars),
        out_specs=[VMEM] * len(shapes) if many else VMEM,
        compiler_params=pltpu.CompilerParams(vmem_limit_bytes=32 * 1024 * 1024),
    )(*operands)


def exchange(value, axis):
    return lax.all_to_all(value, axis, split_axis=0, concat_axis=0, tiled=True)


def on_device(image_emb, text_emb, log_scale, logit_bias):
    of_x, high, of_y, low = (lax.axis_size(a) for a in ("x", "zh", "y", "zl"))
    rows, narrow = image_emb.shape
    of_i = {16: 4, 4: 2}[low]
    near = low // of_i
    of_j = high * near
    group, small = rows // of_i, rows // of_j
    halves = group // small
    wide = low * narrow
    place = (high, low, of_i, of_j)
    inner = (high, low, halves)

    sent = call(functools.partial(split_kernel, place), (high * low, small, LANES), image_emb.T, text_emb.T)
    got = exchange(sent, ("zh", "zl"))
    mine_i, mine_t = call(
        functools.partial(widen_kernel, inner, narrow),
        [(of_y, high * group, wide), (of_x, high * small, wide)],
        got,
    )
    image = exchange(mine_i, "y")
    text = exchange(mine_t, "x")
    partial = call(logits_kernel, (of_y * high * group, of_x * high * small), image, text)
    other = lax.ppermute(partial, "c", [(0, 1), (1, 0)])
    zl = lax.axis_index("zl")
    at = jnp.stack(
        [lax.axis_index("x"), lax.axis_index("y"), zl // near, lax.axis_index("zh") * near + zl % near]
    ).astype(jnp.int32)
    grad_i, grad_t = call(
        functools.partial(grads_kernel, (high, halves, small, rows, of_y)),
        [image.shape, text.shape],
        at, log_scale, logit_bias, partial, other, image, text,
        scalars=3,
    )
    back_i = exchange(grad_i, "y")
    back_t = exchange(grad_t, "x")
    sent = call(functools.partial(narrow_kernel, inner, narrow), (high * low, small, LANES), back_i, back_t)
    got = exchange(sent, ("zh", "zl"))
    out_i, out_t = call(functools.partial(collect_kernel, place), [(narrow, rows), (narrow, rows)], got)
    return (out_i.T, out_t.T)


def program(mesh, sizes):
    fine = Mesh(mesh.devices.reshape(sizes), ("x", "zh", "y", "zl", "c"))
    dp, mp = ("x", "zh", "y"), ("zl", "c")
    return jax.shard_map(
        on_device,
        mesh=fine,
        in_specs=(P(dp, mp), P(dp, mp), P(), P()),
        out_specs=(P(dp, mp), P(dp, mp)),
        check_vma=False,
    )


def solution(mesh):
    return program(mesh, (4, 2, 4, 16, 2))
```

time: 1640 us -> 173 us (0.11)
  the two profiles are of different devices: /device:TPU:8 before, /device:TPU:2 now
where the time goes in v1:
time: 173 us; the launch traced here: 172 us
  blocking collectives  163 us (94%)
  Pallas kernels  3.81 us (2%)
  between operations  2 us (1%)
  starting transfers between devices  1.92 us (1%)
    all_to_all x6, blocking collectives, exchange(): return lax.all_to_all(value, axis, split_axis=0, concat_axis=0, tiled=True)  163 us
    pallas_call x6, Pallas kernels, call(): pl.pallas_call(kernel, out_shape=shapes if many else shapes[0], in_specs=...  3.81 us
  transfers between devices with their start and end apart: 1, of which 0 were waited for; matrix products, arithmetic and copies ran while one was open for 0% of the time, Pallas kernels for 0%

profile of v1, /device:TPU:2, one launch (start us, length us, event | category | flops | bytes accessed | tf_op | source)
XLA Modules:
  0.0 172.4 jit_solution(307333195934584566)
XLA Ops:
  0.6 0.0 copy-start
  0.6 0.7 copy-done
  1.4 0.0 copy-start.1
  1.4 0.7 copy-done.1
  2.1 0.2 shard_map.59
  2.3 71.1 %all_to_all.30.got_ref = f32[32,16,128]{2,1,0:T(8,128)S(1)} all-to-all(f32[32,16,128]{2,1,0:T(8,128)S(1)} %shard_map.59), channel_id=1, replica_groups=mesh['x'=4,'zh'=2,'y'=4,'zl'=16,'c'=2] {'zh','zl'}, dimensions={0} | all-to-all | bytes 524288 | tf_op jit(solution)/shard_map/all_to_all | solution.py:198
  73.3 0.3 shard_map.60
  73.6 10.2 %all_to_all.31.text_ref = f32[4,32,576]{2,1,0:T(8,128)S(1)} all-to-all(f32[4,32,576]{2,1,0:T(8,128)S(1)} %get-tuple-element.9), channel_id=1, replica_groups=mesh['x'=4,'zh'=2,'y'=4,'zl'=16,'c'=2] {'x'}, dimensions={0} | all-to-all | bytes 589824 | tf_op jit(solution)/shard_map/all_to_all | solution.py:198
  83.8 13.0 %all_to_all.32.image_ref = f32[4,64,576]{2,1,0:T(8,128)S(1)} all-to-all(f32[4,64,576]{2,1,0:T(8,128)S(1)} %get-tuple-element.8), channel_id=1, replica_groups=mesh['x'=4,'zh'=2,'y'=4,'zl'=16,'c'=2] {'y'}, dimensions={0} | all-to-all | bytes 1179648 | tf_op jit(solution)/shard_map/all_to_all | solution.py:198
  96.8 0.7 shard_map.61.mine_ref
  97.5 1.9 %collective-permute-start = (f32[256,128]{1,0:T(8,128)S(1)}, f32[256,128]{1,0:T(8,128)S(1)}, u32[]{:S(2)}, u32[]{:S(2)}) collective-permute-start(f32[256,128]{1,0:T(8,128)S(1)} %shard_map.61.mine_ref), channel_id=1, source_target_pairs={{0,1},{1,0},{2,3},{3,2},{4,5},{5,4},{6,7},{7,6},{8,9},{9,8},{10,11... | collective-permute-start | bytes 393224 | tf_op jit(solution)/shard_map/ppermute | solution.py:223
  100.8 0.1 pad_add_fusion.at_ref
  100.9 0.0 collective-permute-done.other_ref
  100.9 1.6 shard_map.62
  102.5 10.7 %all_to_all.33.text_ref = f32[4,32,576]{2,1,0:T(8,128)S(1)} all-to-all(f32[4,32,576]{2,1,0:T(8,128)S(1)} %get-tuple-element.11), channel_id=1, replica_groups=mesh['x'=4,'zh'=2,'y'=4,'zl'=16,'c'=2] {'x'}, dimensions={0} | all-to-all | bytes 589824 | tf_op jit(solution)/shard_map/all_to_all | solution.py:198
  113.2 13.4 %all_to_all.34.image_ref = f32[4,64,576]{2,1,0:T(8,128)S(1)} all-to-all(f32[4,64,576]{2,1,0:T(8,128)S(1)} %get-tuple-element.10), channel_id=1, replica_groups=mesh['x'=4,'zh'=2,'y'=4,'zl'=16,'c'=2] {'y'}, dimensions={0} | all-to-all | bytes 1179648 | tf_op jit(solution)/shard_map/all_to_all | solution.py:198
  126.6 0.3 shard_map.63
  126.9 44.8 %all_to_all.35.got_ref = f32[32,16,128]{2,1,0:T(8,128)S(1)} all-to-all(f32[32,16,128]{2,1,0:T(8,128)S(1)} %shard_map.63), channel_id=1, replica_groups=mesh['x'=4,'zh'=2,'y'=4,'zl'=16,'c'=2] {'zh','zl'}, dimensions={0} | all-to-all | bytes 524288 | tf_op jit(solution)/shard_map/all_to_all | solution.py:198
  171.7 0.8 shard_map.64
Async XLA Ops:
  0.6 0.7 copy-start
  1.4 0.7 copy-start.1
  97.5 3.3 %collective-permute-start = (f32[256,128]{1,0:T(8,128)S(1)}, f32[256,128]{1,0:T(8,128)S(1)}, u32[]{:S(2)}, u32[]{:S(2)}) collective-permute-start(f32[256,128]{1,0:T(8,128)S(1)} %shard_map.61.mine_ref), channel_id=1, source_target_pairs={{0,1},{1,0},{2,3},{3,2},{4,5},{5,4},{6,7},{7,6},{8,9},{9,8},{10,11... | collective-permute-start | bytes 393224 | tf_op jit(solution)/shard_map/ppermute | solution.py:223

commit v2 on v0

v2 whole, which is shorter than its diff:
```python
import functools

import jax
import jax.numpy as jnp
from jax import lax
from jax.experimental import pallas as pl
from jax.experimental.pallas import tpu as pltpu
from jax.sharding import Mesh, PartitionSpec as P

LANES = 128
SUB = 8
VMEM = pl.BlockSpec(memory_space=pltpu.VMEM)
SMEM = pl.BlockSpec(memory_space=pltpu.SMEM)


def rows_first(block):
    narrow, rows = block.shape
    filled = jnp.concatenate([block, jnp.zeros((LANES - narrow, rows), block.dtype)], axis=0)
    return filled.T


def shift(block, lanes):
    lanes = lanes % LANES
    return block if lanes == 0 else pltpu.roll(block, lanes, 1)


def take(tiles, at, width):
    tile, off = divmod(at, LANES)
    value = shift(tiles[tile], -off)
    lane = lax.broadcasted_iota(jnp.int32, value.shape, 1)
    if off + width > LANES:
        value = jnp.where(lane < LANES - off, value, shift(tiles[tile + 1], -off))
    return jnp.where(lane < width, value, 0.0)


def put(tiles, at, width, value):
    tile, off = divmod(at, LANES)
    moved = shift(value, off)
    pieces = [(tile, moved)]
    if off + width > LANES:
        lane = lax.broadcasted_iota(jnp.int32, value.shape, 1)
        pieces = [(tile, jnp.where(lane >= off, moved, 0.0)), (tile + 1, jnp.where(lane < off, moved, 0.0))]
    for which, part in pieces:
        tiles[which] = part if tiles[which] is None else tiles[which] + part


def load(ref, first, start, rows, width):
    found = []
    for lo in range(0, width, LANES):
        hi = min(lo + LANES, width)
        value = ref[first, start : start + rows, lo:hi]
        if hi - lo < LANES:
            value = jnp.concatenate([value, jnp.zeros((rows, LANES - hi + lo), value.dtype)], axis=1)
        found.append(value)
    return found


def store(ref, index, start, tiles, width):
    rows = tiles[0].shape[0]
    for tile, value in enumerate(tiles):
        lo = tile * LANES
        hi = min(lo + LANES, width)
        if index is None:
            ref[start : start + rows, lo:hi] = value[:, : hi - lo]
        else:
            ref[index, start : start + rows, lo:hi] = value[:, : hi - lo]


def tiles_of(lanes):
    return -(-lanes // LANES)


def filled(tiles):
    shape = next(t.shape for t in tiles if t is not None)
    return [jnp.zeros(shape, jnp.float32) if t is None else t for t in tiles]


def split_kernel(of_i, of_j, image_ref, text_ref, out_ref):
    narrow, rows = image_ref.shape
    image, text = rows_first(image_ref[...]), rows_first(text_ref[...])
    blocks_i, blocks_j = rows // of_i // SUB, rows // of_j // SUB
    width = out_ref.shape[2]

    def packed(block, first, count, lane_block):
        tiles = [None] * tiles_of(width)
        for k in range(count):
            start = (first + k) * SUB
            put(tiles, (lane_block + k) * narrow, narrow, block[start : start + SUB])
        return tiles

    images = [packed(image, i * blocks_i, blocks_i, 0) for i in range(of_i)]
    texts = [packed(text, j * blocks_j, blocks_j, blocks_i) for j in range(of_j)]
    for j in range(of_j):
        for i in range(of_i):
            tiles = [
                a if b is None else b if a is None else a + b for a, b in zip(images[i], texts[j])
            ]
            store(out_ref, j * of_i + i, 0, filled(tiles), width)


def widen_kernel(sizes, narrow, got_ref, image_ref, text_ref):
    of_i, of_j, blocks_i, blocks_j = sizes
    copies, _, wide = image_ref.shape
    rows = [[load(got_ref, j * of_i + i, 0, SUB, got_ref.shape[2]) for i in range(of_i)] for j in range(of_j)]
    for j in range(of_j):
        for k in range(blocks_i + blocks_j):
            tiles = [None] * tiles_of(wide)
            for i in range(of_i):
                put(tiles, i * narrow, narrow, take(rows[j][i], k * narrow, narrow))
            if k < blocks_i:
                for copy in range(copies):
                    store(image_ref, copy, (j * blocks_i + k) * SUB, tiles, wide)
            else:
                store(text_ref, None, (j * blocks_j + k - blocks_i) * SUB, tiles, wide)


def logits_kernel(image_ref, text_ref, out_ref):
    a, m, w = image_ref.shape
    out_ref[...] = lax.dot_general(
        image_ref[...].reshape(a * m, w),
        text_ref[...],
        (((1,), (1,)), ((), ())),
        preferred_element_type=jnp.float32,
        precision=lax.Precision.HIGHEST,
    )


def grads_kernel(sizes, at_ref, log_scale_ref, bias_ref, sums_ref, image_ref, text_ref, gi_ref, gt_ref):
    high, of_y, rows, group_i, group_j = sizes
    a, m, w = image_ref.shape
    scale = jnp.exp(jnp.full((1, 1), log_scale_ref[0], jnp.float32))
    logits = scale * (sums_ref[0] + sums_ref[1]) + bias_ref[0]
    x, y, i, j = at_ref[0], at_ref[1], at_ref[2], at_ref[3]
    r = lax.broadcasted_iota(jnp.int32, logits.shape, 0)
    source, zh, inner = r // m, (r % m) // group_i, r % group_i
    row_ids = ((source // of_y * high + zh) * of_y + source % of_y) * rows + i * group_i + inner
    c = lax.broadcasted_iota(jnp.int32, logits.shape, 1)
    zh, inner = c // group_j, c % group_j
    col_ids = ((x * high + zh) * of_y + y) * rows + j * group_j + inner
    label = jnp.where(row_ids == col_ids, 1.0, -1.0)
    coef = -label * jax.nn.sigmoid(-label * logits)
    dot = functools.partial(
        lax.dot_general, preferred_element_type=jnp.float32, precision=lax.Precision.HIGHEST
    )
    gi_ref[...] = (scale * dot(coef, text_ref[...], (((1,), (0,)), ((), ())))).reshape(a, m, w)
    gt_ref[...] = scale * dot(coef, image_ref[...].reshape(a * m, w), (((0,), (0,)), ((), ())))


def narrow_kernel(sizes, narrow, image_ref, text_ref, out_ref):
    of_i, of_j, blocks_i, blocks_j = sizes
    copies, _, wide = image_ref.shape
    width = out_ref.shape[2]
    for j in range(of_j):
        rows = []
        for k in range(blocks_i):
            start = (j * blocks_i + k) * SUB
            tiles = load(image_ref, 0, start, SUB, wide)
            for copy in range(1, copies):
                tiles = [a + b for a, b in zip(tiles, load(image_ref, copy, start, SUB, wide))]
            rows.append(tiles)
        for k in range(blocks_j):
            rows.append(load(text_ref, 0, (j * blocks_j + k) * SUB, SUB, wide))
        for i in range(of_i):
            tiles = [None] * tiles_of(width)
            for k, value in enumerate(rows):
                put(tiles, k * narrow, narrow, take(value, i * narrow, narrow))
            store(out_ref, j * of_i + i, 0, tiles, width)


def collect_kernel(sizes, got_ref, image_ref, text_ref):
    of_i, of_j, blocks_i, blocks_j = sizes
    narrow, rows = image_ref.shape
    width = got_ref.shape[2]

    def total(sources):
        tiles = load(got_ref, sources[0], 0, SUB, width)
        for source in sources[1:]:
            tiles = [a + b for a, b in zip(tiles, load(got_ref, source, 0, SUB, width))]
        return tiles

    images, texts = [], []
    for i in range(of_i):
        tiles = total([j * of_i + i for j in range(of_j)])
        images += [take(tiles, k * narrow, narrow) for k in range(blocks_i)]
    for j in range(of_j):
        tiles = total([j * of_i + i for i in range(of_i)])
        texts += [take(tiles, (blocks_i + k) * narrow, narrow) for k in range(blocks_j)]
    image_ref[...] = jnp.concatenate(images, axis=0).T[:narrow]
    text_ref[...] = jnp.concatenate(texts, axis=0).T[:narrow]


def call(kernel, outs, *operands, scalars=0):
    many = isinstance(outs, list)
    shapes = [jax.ShapeDtypeStruct(s, jnp.float32) for s in (outs if many else [outs])]
    return pl.pallas_call(
        kernel,
        out_shape=shapes if many else shapes[0],
        in_specs=[SMEM] * scalars + [VMEM] * (len(operands) - scalars),
        out_specs=[VMEM] * len(shapes) if many else VMEM,
        compiler_params=pltpu.CompilerParams(vmem_limit_bytes=32 * 1024 * 1024),
    )(*operands)


def exchange(value, axis):
    return lax.all_to_all(value, axis, split_axis=0, concat_axis=0, tiled=True)


def on_device(image_emb, text_emb, log_scale, logit_bias):
    of_x, of_j, of_y, of_i = (lax.axis_size(a) for a in ("x", "zh", "y", "zm"))
    rows, narrow = image_emb.shape
    group_i, group_j = rows // of_i, rows // of_j
    blocks = (of_i, of_j, group_i // SUB, group_j // SUB)
    wide = of_i * narrow
    packed = (of_j * of_i, SUB, tiles_of((group_i + group_j) // SUB * narrow) * LANES)

    sent = call(functools.partial(split_kernel, of_i, of_j), packed, image_emb.T, text_emb.T)
    got = exchange(sent, ("zh", "zm"))
    mine, text = call(
        functools.partial(widen_kernel, blocks, narrow),
        [(of_x * of_y, of_j * group_i, wide), (of_j * group_j, wide)],
        got,
    )
    image = exchange(mine, ("x", "y"))
    part = call(logits_kernel, (of_x * of_y * of_j * group_i, of_j * group_j), image, text)
    part = part + lax.ppermute(part, "ze", [(0, 1), (1, 0)])
    sums = lax.all_gather(part, "c")
    at = jnp.stack([lax.axis_index(a) for a in ("x", "y", "zm", "zh")]).astype(jnp.int32)
    grad_i, grad_t = call(
        functools.partial(grads_kernel, (of_j, of_y, rows, group_i, group_j)),
        [image.shape, text.shape],
        at, log_scale, logit_bias, sums, image, text,
        scalars=3,
    )
    back = exchange(grad_i, ("x", "y"))
    sent = call(functools.partial(narrow_kernel, blocks, narrow), packed, back, grad_t[None])
    got = exchange(sent, ("zh", "zm"))
    out_i, out_t = call(functools.partial(collect_kernel, blocks), [(narrow, rows), (narrow, rows)], got)
    return (out_i.T, out_t.T)


def program(mesh, sizes):
    x, zh, y, zl, c = sizes
    fine = Mesh(mesh.devices.reshape(x, zh, y, zl // 2, 2, c), ("x", "zh", "y", "zm", "ze", "c"))
    dp, mp = ("x", "zh", "y"), ("zm", "ze", "c")
    return jax.shard_map(
        on_device,
        mesh=fine,
        in_specs=(P(dp, mp), P(dp, mp), P(), P()),
        out_specs=(P(dp, mp), P(dp, mp)),
        check_vma=False,
    )


def solution(mesh):
    return program(mesh, (4, 2, 4, 16, 2))
```

time: 1640 us -> 157 us (0.10)
  the two profiles are of different devices: /device:TPU:8 before, /device:TPU:66 now
where the time goes in v2:
time: 157 us; the launch traced here: 156 us
  blocking collectives  138 us (88%)
  Pallas kernels  7.81 us (5%)
  waiting for transfers between devices  4.06 us (3%)
  starting transfers between devices  2.82 us (2%)
  between operations  1.98 us (1%)
    all_to_all x4, blocking collectives, exchange(): return lax.all_to_all(value, axis, split_axis=0, concat_axis=0, tiled=True)  136 us
    pallas_call x6, Pallas kernels, call(): pl.pallas_call(kernel, out_shape=shapes if many else shapes[0], in_specs=...  7.81 us
    ppermute x1, waiting for transfers between devices, on_device(): part = part + lax.ppermute(part, 'ze', [(0, 1), (1, 0)])  4.06 us
  transfers between devices with their start and end apart: 1, of which 1 were waited for; matrix products, arithmetic and copies ran while one was open for 0% of the time, Pallas kernels for 0%

profile of v2, /device:TPU:66, one launch (start us, length us, event | category | flops | bytes accessed | tf_op | source)
XLA Modules:
  0.0 156.4 jit_solution(12797398804371588688)
XLA Ops:
  0.6 0.0 copy-start
  0.6 0.7 copy-done
  1.4 0.0 copy-start.1
  1.4 0.7 copy-done.1
  2.1 0.2 shard_map.59
  2.3 57.9 %all_to_all.20.got_ref = f32[16,8,384]{2,1,0:T(8,128)S(1)} all-to-all(f32[16,8,384]{2,1,0:T(8,128)S(1)} %shard_map.59), channel_id=1, replica_groups=mesh['x'=4,'zh'=2,'y'=4,'zm'=8,'ze'=2,'c'=2] {'zh','zm'}, dimensions={0} | all-to-all | bytes 393216 | tf_op jit(solution)/shard_map/all_to_all | solution.py:205
  60.2 2.0 %shard_map.60 = (f32[16,32,288]{2,1,0:T(8,128)S(1)}, f32[128,288]{1,0:T(8,128)S(1)}) custom-call(f32[16,8,384]{2,1,0:T(8,128)S(1)} %all_to_all.20.got_ref), custom_call_target="tpu_custom_call" | custom-call | tf_op jit(solution)/shard_map/pallas_call | solution.py:195
  62.2 19.1 %all_to_all.21.image_ref = f32[16,32,288]{2,1,0:T(8,128)S(1)} all-to-all(f32[16,32,288]{2,1,0:T(8,128)S(1)} %get-tuple-element.8), channel_id=1, replica_groups=mesh['x'=4,'zh'=2,'y'=4,'zm'=8,'ze'=2,'c'=2] {'x','y'}, dimensions={0} | all-to-all | bytes 1179648 | tf_op jit(solution)/shard_map/all_to_all | solution.py:205
  81.2 0.8 shard_map.61
  82.0 2.8 %collective-permute-start = (f32[512,128]{1,0:T(8,128)S(1)}, f32[512,128]{1,0:T(8,128)S(1)}, u32[]{:S(2)}, u32[]{:S(2)}) collective-permute-start(f32[512,128]{1,0:T(8,128)S(1)} %shard_map.61), channel_id=1, source_target_pairs={{0,2},{2,0},{1,3},{3,1},{4,6},{6,4},{5,7},{7,5},{8,10},{10,8},{9,1... | collective-permute-start | bytes 786440 | tf_op jit(solution)/shard_map/ppermute | solution.py:225
  86.1 0.1 pad_add_fusion.at_ref
  86.2 4.1 %collective-permute-done = f32[512,128]{1,0:T(8,128)S(1)} collective-permute-done((f32[512,128]{1,0:T(8,128)S(1)}, f32[512,128]{1,0:T(8,128)S(1)}, u32[]{:S(2)}, u32[]{:S(2)}) %collective-permute-start) | collective-permute-done | bytes 262176 | tf_op jit(solution)/shard_map/ppermute | solution.py:225
  90.3 2.2 %all-gather = f32[1024,128]{1,0:T(8,128)S(1)} all-gather(f32[512,128]{1,0:T(8,128)S(1)} %add.3), channel_id=2, replica_groups=mesh['x'=4,'zh'=2,'y'=4,'zm'=8,'ze'=2,'c'=2] {'c'}, dimensions={0}, use_global_device_ids=true | all-gather | bytes 786432 | tf_op jit(solution)/shard_map/all_gather | solution.py:226
  92.5 1.9 %shard_map.62 = (f32[16,32,288]{2,1,0:T(8,128)S(1)}, f32[128,288]{1,0:T(8,128)S(1)}) custom-call(s32[4]{0:T(128)S(1)} %pad_add_fusion.at_ref, f32[1]{0:T(128)S(6)} %copy.6.log_scale_ref, f32[1]{0:T(128)S(6)} %copy.7.bias_ref, f32[2,512,128]{2,1,0:T(8,128)S(1)} %bitcast.10, f32[16,32,288]{2,1,0:T(8,128)S(1)} %all_to_all.21.image_ref, ...), custom_call_target="tpu_custom_call" | custom-call | tf_op jit(solution)/shard_map/pallas_call | solution.py:195
  94.4 17.8 %all_to_all.22.image_ref = f32[16,32,288]{2,1,0:T(8,128)S(1)} all-to-all(f32[16,32,288]{2,1,0:T(8,128)S(1)} %get-tuple-element.10), channel_id=1, replica_groups=mesh['x'=4,'zh'=2,'y'=4,'zm'=8,'ze'=2,'c'=2] {'x','y'}, dimensions={0} | all-to-all | bytes 1179648 | tf_op jit(solution)/shard_map/all_to_all | solution.py:205
  112.3 2.2 %shard_map.63 = f32[16,8,384]{2,1,0:T(8,128)S(1)} custom-call(f32[16,32,288]{2,1,0:T(8,128)S(1)} %all_to_all.22.image_ref, f32[1,128,288]{2,1,0:T(8,128)S(1)} %bitcast.11), custom_call_target="tpu_custom_call" | custom-call | tf_op jit(solution)/shard_map/pallas_call | solution.py:195
  114.5 41.2 %all_to_all.23.got_ref = f32[16,8,384]{2,1,0:T(8,128)S(1)} all-to-all(f32[16,8,384]{2,1,0:T(8,128)S(1)} %shard_map.63), channel_id=1, replica_groups=mesh['x'=4,'zh'=2,'y'=4,'zm'=8,'ze'=2,'c'=2] {'zh','zm'}, dimensions={0} | all-to-all | bytes 393216 | tf_op jit(solution)/shard_map/all_to_all | solution.py:205
  155.7 0.8 shard_map.64
  (1 shorter events, 0.0 us)
Async XLA Ops:
  0.6 0.7 copy-start
  1.4 0.7 copy-start.1
  82.0 8.3 %collective-permute-start = (f32[512,128]{1,0:T(8,128)S(1)}, f32[512,128]{1,0:T(8,128)S(1)}, u32[]{:S(2)}, u32[]{:S(2)}) collective-permute-start(f32[512,128]{1,0:T(8,128)S(1)} %shard_map.61), channel_id=1, source_target_pairs={{0,2},{2,0},{1,3},{3,1},{4,6},{6,4},{5,7},{7,5},{8,10},{10,8},{9,1... | collective-permute-start | bytes 786440 | tf_op jit(solution)/shard_map/ppermute | solution.py:225

commit v3 on v2

v3 whole, which is shorter than its diff:
```python
import functools

import jax
import jax.numpy as jnp
from jax import lax
from jax.experimental import pallas as pl
from jax.experimental.pallas import tpu as pltpu
from jax.sharding import Mesh, PartitionSpec as P

LANES = 128
SUB = 8
VMEM = pl.BlockSpec(memory_space=pltpu.VMEM)
SMEM = pl.BlockSpec(memory_space=pltpu.SMEM)


def rows_first(block):
    narrow, rows = block.shape
    filled = jnp.concatenate([block, jnp.zeros((LANES - narrow, rows), block.dtype)], axis=0)
    return filled.T


def shift(block, lanes):
    lanes = lanes % LANES
    return block if lanes == 0 else pltpu.roll(block, lanes, 1)


def tiles_of(lanes):
    return -(-lanes // LANES)


def lanes_from(off, shape):
    return lax.broadcasted_iota(jnp.int32, shape, 1) >= off


def pick(tile, at, width, to):
    which, off = divmod(at, LANES)
    value = tile(which)
    if off + width <= LANES:
        return shift(value, to - off)
    first, second = shift(value, -off), shift(tile(which + 1), -off)
    return shift(jnp.where(lanes_from(LANES - off, value.shape), second, first), to)


def packed(blocks, width):
    tiles = [None] * tiles_of(len(blocks) * width)
    for k, (tile, at) in enumerate(blocks):
        which, off = divmod(k * width, LANES)
        value = pick(tile, at, width, off)
        tiles[which] = value if tiles[which] is None else jnp.where(lanes_from(off, value.shape), value, tiles[which])
        if off + width > LANES:
            tiles[which + 1] = value
    return tiles


def reader(ref, first, start=0):
    def tile(which):
        lanes = slice(which * LANES, (which + 1) * LANES)
        if first is None:
            return ref[start : start + SUB, lanes]
        return ref[first, start : start + SUB, lanes]

    return tile


def split_kernel(of_i, of_j, image_any, text_any, out_ref, image_ref, text_ref, sems):
    copies = [
        pltpu.make_async_copy(image_any, image_ref, sems.at[0]),
        pltpu.make_async_copy(text_any, text_ref, sems.at[1]),
    ]
    for copy in copies:
        copy.start()
    for copy in copies:
        copy.wait()
    narrow, rows = image_ref.shape
    image, text = rows_first(image_ref[...]), rows_first(text_ref[...])
    blocks_i, blocks_j = rows // of_i // SUB, rows // of_j // SUB

    def block(rows_of, index):
        value = rows_of[index * SUB : (index + 1) * SUB]
        return (lambda which: value, 0)

    for j in range(of_j):
        texts = [block(text, j * blocks_j + k) for k in range(blocks_j)]
        for i in range(of_i):
            images = [block(image, i * blocks_i + k) for k in range(blocks_i)]
            for which, value in enumerate(packed(images + texts, narrow)):
                out_ref[j * of_i + i, :, which * LANES : (which + 1) * LANES] = value


def widen_kernel(sizes, narrow, got_ref, image_ref, text_ref):
    of_i, of_j, blocks_i, blocks_j = sizes
    copies = image_ref.shape[0]
    full, rest = divmod(of_i * narrow, LANES)
    last = None
    for j in range(of_j):
        sources = [reader(got_ref, j * of_i + i) for i in range(of_i)]
        for k in range(blocks_i + blocks_j):
            tiles = packed([(source, k * narrow) for source in sources], narrow)
            if k < blocks_i:
                group = j * blocks_i + k
                for copy in range(copies):
                    for which in range(full):
                        lo = (group * full + which) * LANES
                        image_ref[copy, :, lo : lo + LANES] = tiles[which]
                moved = shift(tiles[full], group * rest)
                last = moved if last is None else jnp.where(lanes_from(group * rest, moved.shape), moved, last)
            else:
                at = (j * blocks_j + k - blocks_i) * SUB
                tiles[full] = jnp.where(lanes_from(rest, tiles[full].shape), 0.0, tiles[full])
                for which, value in enumerate(tiles):
                    text_ref[at : at + SUB, which * LANES : (which + 1) * LANES] = value
    lo = of_j * blocks_i * full * LANES
    for copy in range(copies):
        image_ref[copy, :, lo : lo + LANES] = last


def stacked(image_ref, groups, full, rest):
    sources = image_ref.shape[0]
    lo = groups * full * LANES
    last = image_ref[:, :, lo : lo + LANES].reshape(sources * SUB, LANES)
    found = []
    for group in range(groups):
        at = group * full * LANES
        whole = image_ref[:, :, at : at + full * LANES].reshape(sources * SUB, full * LANES)
        found.append(jnp.concatenate([whole, shift(last, -group * rest)], axis=1))
    return jnp.concatenate(found, axis=0)


dot = functools.partial(
    lax.dot_general, preferred_element_type=jnp.float32, precision=lax.Precision.HIGHEST
)


def logits_kernel(tiling, image_ref, text_ref, out_ref):
    out_ref[...] = dot(stacked(image_ref, *tiling), text_ref[...], (((1,), (1,)), ((), ())))


def grads_kernel(sizes, tiling, at_ref, log_scale_ref, bias_ref, own_ref, far_ref, image_ref, text_ref, gi_ref, gt_ref):
    high, of_y, rows, group_i, group_j = sizes
    groups, full, rest = tiling
    sources = image_ref.shape[0]
    scale = jnp.exp(jnp.full((1, 1), log_scale_ref[0], jnp.float32))
    logits = scale * ((own_ref[0] + own_ref[1]) + (far_ref[0] + far_ref[1])) + bias_ref[0]
    x, y, i, j = at_ref[0], at_ref[1], at_ref[2], at_ref[3]
    r = lax.broadcasted_iota(jnp.int32, logits.shape, 0)
    group, source = r // (sources * SUB), r % (sources * SUB) // SUB
    blocks_i = group_i // SUB
    zh, inner = group // blocks_i, group % blocks_i * SUB + r % SUB
    row_ids = ((source // of_y * high + zh) * of_y + source % of_y) * rows + i * group_i + inner
    c = lax.broadcasted_iota(jnp.int32, logits.shape, 1)
    zh, inner = c // group_j, c % group_j
    col_ids = ((x * high + zh) * of_y + y) * rows + j * group_j + inner
    label = jnp.where(row_ids == col_ids, 1.0, -1.0)
    coef = -label * jax.nn.sigmoid(-label * logits)
    found = scale * dot(coef, text_ref[...], (((1,), (0,)), ((), ())))
    last = None
    for group in range(groups):
        part = found[group * sources * SUB : (group + 1) * sources * SUB]
        at = group * full * LANES
        gi_ref[:, :, at : at + full * LANES] = part[:, : full * LANES].reshape(sources, SUB, full * LANES)
        moved = shift(part[:, full * LANES :], group * rest)
        last = moved if last is None else last + moved
    lo = groups * full * LANES
    gi_ref[:, :, lo : lo + LANES] = last.reshape(sources, SUB, LANES)
    gt_ref[...] = scale * dot(coef, stacked(image_ref, *tiling), (((0,), (0,)), ((), ())))


def narrow_kernel(sizes, narrow, image_ref, text_ref, out_ref):
    of_i, of_j, blocks_i, blocks_j = sizes
    full, rest = divmod(of_i * narrow, LANES)
    total = image_ref[0]
    for copy in range(1, image_ref.shape[0]):
        total = total + image_ref[copy]
    lo = of_j * blocks_i * full
    tiles = [total[:, k * LANES : (k + 1) * LANES] for k in range(lo + 1)]

    def image_row(group):
        row = tiles[group * full : (group + 1) * full] + [shift(tiles[lo], -group * rest)]
        return lambda which: row[which]

    for j in range(of_j):
        rows = [image_row(j * blocks_i + k) for k in range(blocks_i)]
        rows += [reader(text_ref, None, (j * blocks_j + k) * SUB) for k in range(blocks_j)]
        for i in range(of_i):
            for which, value in enumerate(packed([(row, i * narrow) for row in rows], narrow)):
                out_ref[j * of_i + i, :, which * LANES : (which + 1) * LANES] = value


def collect_kernel(sizes, got_ref, image_ref, text_ref):
    of_i, of_j, blocks_i, blocks_j = sizes
    narrow = image_ref.shape[0]

    def total(sources, first, last):
        tiles = {}
        for which in range(first * narrow // LANES, tiles_of(last * narrow)):
            tiles[which] = reader(got_ref, sources[0])(which)
            for source in sources[1:]:
                tiles[which] = tiles[which] + reader(got_ref, source)(which)
        return [pick(lambda which: tiles[which], k * narrow, narrow, 0) for k in range(first, last)]

    images, texts = [], []
    for i in range(of_i):
        images += total([j * of_i + i for j in range(of_j)], 0, blocks_i)
    for j in range(of_j):
        texts += total([j * of_i + i for i in range(of_i)], blocks_i, blocks_i + blocks_j)
    image_ref[...] = jnp.concatenate(images, axis=0).T[:narrow]
    text_ref[...] = jnp.concatenate(texts, axis=0).T[:narrow]


def call(kernel, outs, *operands, scalars=0, inputs=VMEM, scratch=()):
    many = isinstance(outs, list)
    shapes = [jax.ShapeDtypeStruct(s, jnp.float32) for s in (outs if many else [outs])]
    return pl.pallas_call(
        kernel,
        out_shape=shapes if many else shapes[0],
        in_specs=[SMEM] * scalars + [inputs] * (len(operands) - scalars),
        out_specs=[VMEM] * len(shapes) if many else VMEM,
        scratch_shapes=list(scratch),
        compiler_params=pltpu.CompilerParams(vmem_limit_bytes=32 * 1024 * 1024),
    )(*operands)


def exchange(value, axis):
    return lax.all_to_all(value, axis, split_axis=0, concat_axis=0, tiled=True)


def on_device(image_emb, text_emb, log_scale, logit_bias):
    of_x, of_j, of_y, of_i = (lax.axis_size(a) for a in ("x", "zh", "y", "zm"))
    rows, narrow = image_emb.shape
    group_i, group_j = rows // of_i, rows // of_j
    blocks = (of_i, of_j, group_i // SUB, group_j // SUB)
    full, rest = divmod(of_i * narrow, LANES)
    groups = of_j * blocks[2]
    assert 0 < rest * groups <= LANES
    tiling = (groups, full, rest)
    plane = of_x * of_y
    sent_shape = (of_j * of_i, SUB, tiles_of((blocks[2] + blocks[3]) * narrow) * LANES)
    block = pltpu.VMEM((narrow, rows), jnp.float32)

    sent = call(
        functools.partial(split_kernel, of_i, of_j), sent_shape, image_emb.T, text_emb.T,
        inputs=pl.BlockSpec(memory_space=pl.ANY), scratch=[block, block, pltpu.SemaphoreType.DMA((2,))],
    )
    got = exchange(sent, ("zh", "zm"))
    mine, text = call(
        functools.partial(widen_kernel, blocks, narrow),
        [(plane, SUB, (groups * full + 1) * LANES), (of_j * group_j, (full + 1) * LANES)],
        got,
    )
    image = exchange(mine, ("x", "y"))
    part = call(functools.partial(logits_kernel, tiling), (plane * groups * SUB, of_j * group_j), image, text)
    other = lax.ppermute(part, "ze", [(0, 1), (1, 0)])
    own = lax.all_gather(part, "c")
    far = lax.all_gather(other, "c")
    at = jnp.stack([lax.axis_index(a) for a in ("x", "y", "zm", "zh")]).astype(jnp.int32)
    grad_i, grad_t = call(
        functools.partial(grads_kernel, (of_j, of_y, rows, group_i, group_j), tiling),
        [image.shape, text.shape],
        at, log_scale, logit_bias, own, far, image, text,
        scalars=3,
    )
    back = exchange(grad_i, ("x", "y"))
    sent = call(functools.partial(narrow_kernel, blocks, narrow), sent_shape, back, grad_t)
    got = exchange(sent, ("zh", "zm"))
    out_i, out_t = call(functools.partial(collect_kernel, blocks), [(narrow, rows), (narrow, rows)], got)
    return (out_i.T, out_t.T)


def program(mesh, sizes):
    x, zh, y, zl, c = sizes
    fine = Mesh(mesh.devices.reshape(x, zh, y, zl // 2, 2, c), ("x", "zh", "y", "zm", "ze", "c"))
    dp, mp = ("x", "zh", "y"), ("zm", "ze", "c")
    return jax.shard_map(
        on_device,
        mesh=fine,
        in_specs=(P(dp, mp), P(dp, mp), P(), P()),
        out_specs=(P(dp, mp), P(dp, mp)),
        check_vma=False,
    )


def solution(mesh):
    return program(mesh, (4, 2, 4, 16, 2))
```

time: 157 us -> 151 us (0.962)
  the two profiles are of different devices: /device:TPU:66 before, /device:TPU:2 now
where the time goes in v3:
time: 151 us; the launch traced here: 150 us
  blocking collectives  134 us (89%)
  Pallas kernels  6.22 us (4%)
  starting transfers between devices  5.22 us (3%)
  between operations  1.98 us (1%)
    all_to_all x4, blocking collectives, exchange(): return lax.all_to_all(value, axis, split_axis=0, concat_axis=0, tiled=True)  130 us
    pallas_call x6, Pallas kernels, call(): pl.pallas_call(kernel, out_shape=shapes if many else shapes[0], in_specs=...  6.22 us
    ppermute x1, starting transfers between devices, on_device(): other = lax.ppermute(part, 'ze', [(0, 1), (1, 0)])  5.22 us
  transfers between devices with their start and end apart: 1, of which 1 were waited for; matrix products, arithmetic and copies ran while one was open for 0% of the time, Pallas kernels for 0%

profile of v3, /device:TPU:2, one launch (start us, length us, event | category | flops | bytes accessed | tf_op | source)
XLA Modules:
  0.0 150.2 jit_solution(4832056890673296794)
XLA Ops:
  0.6 0.0 copy-start
  0.6 0.7 copy-done
  1.4 0.0 copy-start.1
  1.4 0.7 copy-done.1
  2.1 0.2 shard_map.59
  2.3 55.9 %all_to_all.20.got_ref = f32[16,8,384]{2,1,0:T(8,128)S(1)} all-to-all(f32[16,8,384]{2,1,0:T(8,128)S(1)} %shard_map.59), channel_id=1, replica_groups=mesh['x'=4,'zh'=2,'y'=4,'zm'=8,'ze'=2,'c'=2] {'zh','zm'}, dimensions={0} | all-to-all | bytes 393216 | tf_op jit(solution)/shard_map/all_to_all | solution.py:224
  58.2 1.1 shard_map.60
  59.4 16.3 %all_to_all.21.image_ref = f32[16,8,1152]{2,1,0:T(8,128)S(1)} all-to-all(f32[16,8,1152]{2,1,0:T(8,128)S(1)} %get-tuple-element.8), channel_id=1, replica_groups=mesh['x'=4,'zh'=2,'y'=4,'zm'=8,'ze'=2,'c'=2] {'x','y'}, dimensions={0} | all-to-all | bytes 1179648 | tf_op jit(solution)/shard_map/all_to_all | solution.py:224
  75.7 0.8 shard_map.61
  76.5 5.2 %collective-permute-start = (f32[512,128]{1,0:T(8,128)S(1)}, f32[512,128]{1,0:T(8,128)S(1)}, u32[]{:S(2)}, u32[]{:S(2)}) collective-permute-start(f32[512,128]{1,0:T(8,128)S(1)} %shard_map.61), channel_id=1, source_target_pairs={{0,2},{2,0},{1,3},{3,1},{4,6},{6,4},{5,7},{7,5},{8,10},{10,8},{9,1... | collective-permute-start | bytes 786440 | tf_op jit(solution)/shard_map/ppermute | solution.py:252
  83.0 0.1 pad_add_fusion.at_ref
  83.1 2.2 %all-gather = f32[1024,128]{1,0:T(8,128)S(1)} all-gather(f32[512,128]{1,0:T(8,128)S(1)} %shard_map.61), channel_id=2, replica_groups=mesh['x'=4,'zh'=2,'y'=4,'zm'=8,'ze'=2,'c'=2] {'c'}, dimensions={0}, use_global_device_ids=true | all-gather | bytes 786432 | tf_op jit(solution)/shard_map/all_gather | solution.py:253
  85.3 0.8 collective-permute-done
  86.1 2.2 %all-gather.1 = f32[1024,128]{1,0:T(8,128)S(1)} all-gather(f32[512,128]{1,0:T(8,128)S(1)} %collective-permute-done), channel_id=3, replica_groups=mesh['x'=4,'zh'=2,'y'=4,'zm'=8,'ze'=2,'c'=2] {'c'}, dimensions={0}, use_global_device_ids=true | all-gather | bytes 786432 | tf_op jit(solution)/shard_map/all_gather | solution.py:254
  88.2 2.0 %shard_map.62 = (f32[16,8,1152]{2,1,0:T(8,128)S(1)}, f32[128,384]{1,0:T(8,128)S(1)}) custom-call(s32[4]{0:T(128)S(1)} %pad_add_fusion.at_ref, f32[1]{0:T(128)S(6)} %copy.6.log_scale_ref, f32[1]{0:T(128)S(6)} %copy.7.bias_ref, f32[2,512,128]{2,1,0:T(8,128)S(1)} %bitcast.10, f32[2,512,128]{2,1,0:T(8,128)S(1)} %bitcast.11, ...), custom_call_target="tpu_custom_call" | custom-call | tf_op jit(solution)/shard_map/pallas_call | solution.py:213
  90.3 15.7 %all_to_all.22.image_ref = f32[16,8,1152]{2,1,0:T(8,128)S(1)} all-to-all(f32[16,8,1152]{2,1,0:T(8,128)S(1)} %get-tuple-element.10), channel_id=1, replica_groups=mesh['x'=4,'zh'=2,'y'=4,'zm'=8,'ze'=2,'c'=2] {'x','y'}, dimensions={0} | all-to-all | bytes 1179648 | tf_op jit(solution)/shard_map/all_to_all | solution.py:224
  106.0 1.3 shard_map.63
  107.3 42.1 %all_to_all.23.got_ref = f32[16,8,384]{2,1,0:T(8,128)S(1)} all-to-all(f32[16,8,384]{2,1,0:T(8,128)S(1)} %shard_map.63), channel_id=1, replica_groups=mesh['x'=4,'zh'=2,'y'=4,'zm'=8,'ze'=2,'c'=2] {'zh','zm'}, dimensions={0} | all-to-all | bytes 393216 | tf_op jit(solution)/shard_map/all_to_all | solution.py:224
  149.4 0.8 shard_map.64
Async XLA Ops:
  0.6 0.7 copy-start
  1.4 0.7 copy-start.1
  76.5 9.6 %collective-permute-start = (f32[512,128]{1,0:T(8,128)S(1)}, f32[512,128]{1,0:T(8,128)S(1)}, u32[]{:S(2)}, u32[]{:S(2)}) collective-permute-start(f32[512,128]{1,0:T(8,128)S(1)} %shard_map.61), channel_id=1, source_target_pairs={{0,2},{2,0},{1,3},{3,1},{4,6},{6,4},{5,7},{7,5},{8,10},{10,8},{9,1... | collective-permute-start | bytes 786440 | tf_op jit(solution)/shard_map/ppermute | solution.py:252

commit v4 on v3

--- a/solution.py
+++ b/solution.py
@@ -62,10 +62,10 @@
     return tile
 
 
-def split_kernel(of_i, of_j, image_any, text_any, out_ref, image_ref, text_ref, sems):
+def split_kernel(of_i, of_j, image_hbm, text_hbm, out_ref, image_ref, text_ref, sems):
     copies = [
-        pltpu.make_async_copy(image_any, image_ref, sems.at[0]),
-        pltpu.make_async_copy(text_any, text_ref, sems.at[1]),
+        pltpu.make_async_copy(image_hbm, image_ref, sems.at[0]),
+        pltpu.make_async_copy(text_hbm, text_ref, sems.at[1]),
     ]
     for copy in copies:
         copy.start()
@@ -135,13 +135,13 @@
     out_ref[...] = dot(stacked(image_ref, *tiling), text_ref[...], (((1,), (1,)), ((), ())))
 
 
-def grads_kernel(sizes, tiling, at_ref, log_scale_ref, bias_ref, own_ref, far_ref, image_ref, text_ref, gi_ref, gt_ref):
+def grads_kernel(sizes, tiling, log_scale_ref, bias_ref, both_ref, image_ref, text_ref, gi_ref, gt_ref):
     high, of_y, rows, group_i, group_j = sizes
     groups, full, rest = tiling
     sources = image_ref.shape[0]
     scale = jnp.exp(jnp.full((1, 1), log_scale_ref[0], jnp.float32))
-    logits = scale * ((own_ref[0] + own_ref[1]) + (far_ref[0] + far_ref[1])) + bias_ref[0]
-    x, y, i, j = at_ref[0], at_ref[1], at_ref[2], at_ref[3]
+    logits = scale * (both_ref[0] + both_ref[1]) + bias_ref[0]
+    x, y, i, j = (lax.axis_index(a) for a in ("x", "y", "zm", "zh"))
     r = lax.broadcasted_iota(jnp.int32, logits.shape, 0)
     group, source = r // (sources * SUB), r % (sources * SUB) // SUB
     blocks_i = group_i // SUB
@@ -152,7 +152,8 @@
     col_ids = ((x * high + zh) * of_y + y) * rows + j * group_j + inner
     label = jnp.where(row_ids == col_ids, 1.0, -1.0)
     coef = -label * jax.nn.sigmoid(-label * logits)
-    found = scale * dot(coef, text_ref[...], (((1,), (0,)), ((), ())))
+    coef = scale * coef
+    found = dot(coef, text_ref[...], (((1,), (0,)), ((), ())))
     last = None
     for group in range(groups):
         part = found[group * sources * SUB : (group + 1) * sources * SUB]
@@ -162,7 +163,7 @@
         last = moved if last is None else last + moved
     lo = groups * full * LANES
     gi_ref[:, :, lo : lo + LANES] = last.reshape(sources, SUB, LANES)
-    gt_ref[...] = scale * dot(coef, stacked(image_ref, *tiling), (((0,), (0,)), ((), ())))
+    gt_ref[...] = dot(coef, stacked(image_ref, *tiling), (((0,), (0,)), ((), ())))
 
 
 def narrow_kernel(sizes, narrow, image_ref, text_ref, out_ref):
@@ -207,13 +208,13 @@
     text_ref[...] = jnp.concatenate(texts, axis=0).T[:narrow]
 
 
-def call(kernel, outs, *operands, scalars=0, inputs=VMEM, scratch=()):
+def call(kernel, outs, *operands, inputs=None, scratch=()):
     many = isinstance(outs, list)
     shapes = [jax.ShapeDtypeStruct(s, jnp.float32) for s in (outs if many else [outs])]
     return pl.pallas_call(
         kernel,
         out_shape=shapes if many else shapes[0],
-        in_specs=[SMEM] * scalars + [inputs] * (len(operands) - scalars),
+        in_specs=inputs or [VMEM] * len(operands),
         out_specs=[VMEM] * len(shapes) if many else VMEM,
         scratch_shapes=list(scratch),
         compiler_params=pltpu.CompilerParams(vmem_limit_bytes=32 * 1024 * 1024),
@@ -237,9 +238,11 @@
     sent_shape = (of_j * of_i, SUB, tiles_of((blocks[2] + blocks[3]) * narrow) * LANES)
     block = pltpu.VMEM((narrow, rows), jnp.float32)
 
+    held = [pltpu.with_memory_space_constraint(a.T, pltpu.HBM) for a in (image_emb, text_emb)]
     sent = call(
-        functools.partial(split_kernel, of_i, of_j), sent_shape, image_emb.T, text_emb.T,
-        inputs=pl.BlockSpec(memory_space=pl.ANY), scratch=[block, block, pltpu.SemaphoreType.DMA((2,))],
+        functools.partial(split_kernel, of_i, of_j), sent_shape, *held,
+        inputs=[pl.BlockSpec(memory_space=pltpu.HBM)] * 2,
+        scratch=[block, block, pltpu.SemaphoreType.DMA((2,))],
     )
     got = exchange(sent, ("zh", "zm"))
     mine, text = call(
@@ -250,14 +253,12 @@
     image = exchange(mine, ("x", "y"))
     part = call(functools.partial(logits_kernel, tiling), (plane * groups * SUB, of_j * group_j), image, text)
     other = lax.ppermute(part, "ze", [(0, 1), (1, 0)])
-    own = lax.all_gather(part, "c")
-    far = lax.all_gather(other, "c")
-    at = jnp.stack([lax.axis_index(a) for a in ("x", "y", "zm", "zh")]).astype(jnp.int32)
+    both = lax.all_gather(part + other, "c")
     grad_i, grad_t = call(
         functools.partial(grads_kernel, (of_j, of_y, rows, group_i, group_j), tiling),
         [image.shape, text.shape],
-        at, log_scale, logit_bias, own, far, image, text,
-        scalars=3,
+        log_scale, logit_bias, both, image, text,
+        inputs=[SMEM] * 2 + [VMEM] * 3,
     )
     back = exchange(grad_i, ("x", "y"))
     sent = call(functools.partial(narrow_kernel, blocks, narrow), sent_shape, back, grad_t)

time: 151 us -> 149 us (0.987)
  the two profiles are of different devices: /device:TPU:2 before, /device:TPU:8 now
where the time goes in v4:
time: 149 us
  blocking collectives  132 us (89%)
  Pallas kernels  6.39 us (4%)
  starting transfers between devices  5.21 us (3%)
  waiting for transfers between devices  3.04 us (2%)
  between operations  1.97 us (1%)
    all_to_all x4, blocking collectives, exchange(): return lax.all_to_all(value, axis, split_axis=0, concat_axis=0, tiled=True)  130 us
    pallas_call x6, Pallas kernels, call(): pl.pallas_call(kernel, out_shape=shapes if many else shapes[0], in_specs=...  6.39 us
    ppermute x1, starting transfers between devices, on_device(): other = lax.ppermute(part, 'ze', [(0, 1), (1, 0)])  5.21 us
    ppermute x1, waiting for transfers between devices, on_device(): other = lax.ppermute(part, 'ze', [(0, 1), (1, 0)])  3.04 us
  transfers between devices with their start and end apart: 1, of which 1 were waited for; matrix products, arithmetic and copies ran while one was open for 0% of the time, Pallas kernels for 0%

profile of v4, /device:TPU:8, one launch (start us, length us, event | category | flops | bytes accessed | tf_op | source)
XLA Modules:
  0.0 148.8 jit_solution(9365320385013697299)
XLA Ops:
  0.6 0.9 shard_map.59
  1.6 55.9 %all_to_all.20.got_ref = f32[16,8,384]{2,1,0:T(8,128)S(1)} all-to-all(f32[16,8,384]{2,1,0:T(8,128)S(1)} %shard_map.59), channel_id=1, replica_groups=mesh['x'=4,'zh'=2,'y'=4,'zm'=8,'ze'=2,'c'=2] {'zh','zm'}, dimensions={0} | all-to-all | bytes 393216 | tf_op jit(solution)/shard_map/all_to_all | solution.py:225
  57.5 1.1 shard_map.60
  58.6 16.3 %all_to_all.21.image_ref = f32[16,8,1152]{2,1,0:T(8,128)S(1)} all-to-all(f32[16,8,1152]{2,1,0:T(8,128)S(1)} %get-tuple-element.8), channel_id=1, replica_groups=mesh['x'=4,'zh'=2,'y'=4,'zm'=8,'ze'=2,'c'=2] {'x','y'}, dimensions={0} | all-to-all | bytes 1179648 | tf_op jit(solution)/shard_map/all_to_all | solution.py:225
  74.9 0.8 shard_map.61
  75.7 5.2 %collective-permute-start = (f32[512,128]{1,0:T(8,128)S(1)}, f32[512,128]{1,0:T(8,128)S(1)}, u32[]{:S(2)}, u32[]{:S(2)}) collective-permute-start(f32[512,128]{1,0:T(8,128)S(1)} %shard_map.61), channel_id=1, source_target_pairs={{0,2},{2,0},{1,3},{3,1},{4,6},{6,4},{5,7},{7,5},{8,10},{10,8},{9,1... | collective-permute-start | bytes 786440 | tf_op jit(solution)/shard_map/ppermute | solution.py:255
  82.2 3.0 %collective-permute-done = f32[512,128]{1,0:T(8,128)S(1)} collective-permute-done((f32[512,128]{1,0:T(8,128)S(1)}, f32[512,128]{1,0:T(8,128)S(1)}, u32[]{:S(2)}, u32[]{:S(2)}) %collective-permute-start) | collective-permute-done | bytes 262176 | tf_op jit(solution)/shard_map/ppermute | solution.py:255
  85.3 2.2 %all-gather = f32[1024,128]{1,0:T(8,128)S(1)} all-gather(f32[512,128]{1,0:T(8,128)S(1)} %add.3), channel_id=2, replica_groups=mesh['x'=4,'zh'=2,'y'=4,'zm'=8,'ze'=2,'c'=2] {'c'}, dimensions={0}, use_global_device_ids=true | all-gather | bytes 786432 | tf_op jit(solution)/shard_map/all_gather | solution.py:256
  87.5 1.5 %shard_map.62 = (f32[16,8,1152]{2,1,0:T(8,128)S(1)}, f32[128,384]{1,0:T(8,128)S(1)}) custom-call(f32[1]{0:T(128)S(6)} %copy.6.log_scale_ref, f32[1]{0:T(128)S(6)} %copy.7.bias_ref, f32[2,512,128]{2,1,0:T(8,128)S(1)} %bitcast.5, f32[16,8,1152]{2,1,0:T(8,128)S(1)} %all_to_all.21.image_ref, f32[128,384]{1,0:T(8,128)S(1)} %get-tuple-element.9.text_ref), custom_call_target="tpu_custom_call" | custom-call | tf_op jit(solution)/shard_map/pallas_call | solution.py:214
  89.0 15.7 %all_to_all.22.image_ref = f32[16,8,1152]{2,1,0:T(8,128)S(1)} all-to-all(f32[16,8,1152]{2,1,0:T(8,128)S(1)} %get-tuple-element.10), channel_id=1, replica_groups=mesh['x'=4,'zh'=2,'y'=4,'zm'=8,'ze'=2,'c'=2] {'x','y'}, dimensions={0} | all-to-all | bytes 1179648 | tf_op jit(solution)/shard_map/all_to_all | solution.py:225
  104.8 1.3 shard_map.63
  106.0 42.0 %all_to_all.23.got_ref = f32[16,8,384]{2,1,0:T(8,128)S(1)} all-to-all(f32[16,8,384]{2,1,0:T(8,128)S(1)} %shard_map.63), channel_id=1, replica_groups=mesh['x'=4,'zh'=2,'y'=4,'zm'=8,'ze'=2,'c'=2] {'zh','zm'}, dimensions={0} | all-to-all | bytes 393216 | tf_op jit(solution)/shard_map/all_to_all | solution.py:225
  148.1 0.8 shard_map.64
  (1 shorter events, 0.0 us)
Async XLA Ops:
  75.7 9.6 %collective-permute-start = (f32[512,128]{1,0:T(8,128)S(1)}, f32[512,128]{1,0:T(8,128)S(1)}, u32[]{:S(2)}, u32[]{:S(2)}) collective-permute-start(f32[512,128]{1,0:T(8,128)S(1)} %shard_map.61), channel_id=1, source_target_pairs={{0,2},{2,0},{1,3},{3,1},{4,6},{6,4},{5,7},{7,5},{8,10},{10,8},{9,1... | collective-permute-start | bytes 786440 | tf_op jit(solution)/shard_map/ppermute | solution.py:255

commit v5 on v4

--- a/solution.py
+++ b/solution.py
@@ -73,15 +73,15 @@
         copy.wait()
     narrow, rows = image_ref.shape
     image, text = rows_first(image_ref[...]), rows_first(text_ref[...])
-    blocks_i, blocks_j = rows // of_i // SUB, rows // of_j // SUB
+    blocks_i, blocks_j = rows // of_i // SUB, rows // of_j // 2 // SUB
 
     def block(rows_of, index):
         value = rows_of[index * SUB : (index + 1) * SUB]
         return (lambda which: value, 0)
 
     for j in range(of_j):
-        texts = [block(text, j * blocks_j + k) for k in range(blocks_j)]
         for i in range(of_i):
+            texts = [block(text, (j * 2 + i % 2) * blocks_j + k) for k in range(blocks_j)]
             images = [block(image, i * blocks_i + k) for k in range(blocks_i)]
             for which, value in enumerate(packed(images + texts, narrow)):
                 out_ref[j * of_i + i, :, which * LANES : (which + 1) * LANES] = value
@@ -131,11 +131,17 @@
 )
 
 
-def logits_kernel(tiling, image_ref, text_ref, out_ref):
-    out_ref[...] = dot(stacked(image_ref, *tiling), text_ref[...], (((1,), (1,)), ((), ())))
-
-
-def grads_kernel(sizes, tiling, log_scale_ref, bias_ref, both_ref, image_ref, text_ref, gi_ref, gt_ref):
+def both_halves(text_ref, pair_ref):
+    return jnp.concatenate([text_ref[...], pair_ref[...]], axis=0)
+
+
+def logits_kernel(tiling, image_ref, text_ref, pair_ref, out_ref):
+    text = both_halves(text_ref, pair_ref)
+    out_ref[...] = dot(stacked(image_ref, *tiling), text, (((1,), (1,)), ((), ())))
+
+
+def grads_kernel(sizes, tiling, log_scale_ref, bias_ref, both_ref, *refs):
+    image_ref, text_ref, pair_ref, gi_ref, gt_ref, gt_pair_ref = refs
     high, of_y, rows, group_i, group_j = sizes
     groups, full, rest = tiling
     sources = image_ref.shape[0]
@@ -148,12 +154,14 @@
     zh, inner = group // blocks_i, group % blocks_i * SUB + r % SUB
     row_ids = ((source // of_y * high + zh) * of_y + source % of_y) * rows + i * group_i + inner
     c = lax.broadcasted_iota(jnp.int32, logits.shape, 1)
-    zh, inner = c // group_j, c % group_j
-    col_ids = ((x * high + zh) * of_y + y) * rows + j * group_j + inner
+    half, of_half = group_j // 2, text_ref.shape[0]
+    which = (i + c // of_half) % 2
+    zh, inner = c % of_half // half, c % half
+    col_ids = ((x * high + zh) * of_y + y) * rows + j * group_j + which * half + inner
     label = jnp.where(row_ids == col_ids, 1.0, -1.0)
     coef = -label * jax.nn.sigmoid(-label * logits)
     coef = scale * coef
-    found = dot(coef, text_ref[...], (((1,), (0,)), ((), ())))
+    found = dot(coef, both_halves(text_ref, pair_ref), (((1,), (0,)), ((), ())))
     last = None
     for group in range(groups):
         part = found[group * sources * SUB : (group + 1) * sources * SUB]
@@ -163,10 +171,12 @@
         last = moved if last is None else last + moved
     lo = groups * full * LANES
     gi_ref[:, :, lo : lo + LANES] = last.reshape(sources, SUB, LANES)
-    gt_ref[...] = dot(coef, stacked(image_ref, *tiling), (((0,), (0,)), ((), ())))
-
-
-def narrow_kernel(sizes, narrow, image_ref, text_ref, out_ref):
+    found = dot(coef, stacked(image_ref, *tiling), (((0,), (0,)), ((), ())))
+    gt_ref[...] = found[:of_half]
+    gt_pair_ref[...] = found[of_half:]
+
+
+def narrow_kernel(sizes, narrow, image_ref, text_ref, pair_ref, out_ref):
     of_i, of_j, blocks_i, blocks_j = sizes
     full, rest = divmod(of_i * narrow, LANES)
     total = image_ref[0]
@@ -179,9 +189,14 @@
         row = tiles[group * full : (group + 1) * full] + [shift(tiles[lo], -group * rest)]
         return lambda which: row[which]
 
+    def text_row(start):
+        own, pair = reader(text_ref, None, start), reader(pair_ref, None, start)
+        row = [own(which) + pair(which) for which in range(full + 1)]
+        return lambda which: row[which]
+
     for j in range(of_j):
         rows = [image_row(j * blocks_i + k) for k in range(blocks_i)]
-        rows += [reader(text_ref, None, (j * blocks_j + k) * SUB) for k in range(blocks_j)]
+        rows += [text_row((j * blocks_j + k) * SUB) for k in range(blocks_j)]
         for i in range(of_i):
             for which, value in enumerate(packed([(row, i * narrow) for row in rows], narrow)):
                 out_ref[j * of_i + i, :, which * LANES : (which + 1) * LANES] = value
@@ -203,7 +218,8 @@
     for i in range(of_i):
         images += total([j * of_i + i for j in range(of_j)], 0, blocks_i)
     for j in range(of_j):
-        texts += total([j * of_i + i for i in range(of_i)], blocks_i, blocks_i + blocks_j)
+        for half in range(2):
+            texts += total([j * of_i + i for i in range(half, of_i, 2)], blocks_i, blocks_i + blocks_j)
     image_ref[...] = jnp.concatenate(images, axis=0).T[:narrow]
     text_ref[...] = jnp.concatenate(texts, axis=0).T[:narrow]
 
@@ -229,7 +245,7 @@
     of_x, of_j, of_y, of_i = (lax.axis_size(a) for a in ("x", "zh", "y", "zm"))
     rows, narrow = image_emb.shape
     group_i, group_j = rows // of_i, rows // of_j
-    blocks = (of_i, of_j, group_i // SUB, group_j // SUB)
+    blocks = (of_i, of_j, group_i // SUB, group_j // 2 // SUB)
     full, rest = divmod(of_i * narrow, LANES)
     groups = of_j * blocks[2]
     assert 0 < rest * groups <= LANES
@@ -247,21 +263,24 @@
     got = exchange(sent, ("zh", "zm"))
     mine, text = call(
         functools.partial(widen_kernel, blocks, narrow),
-        [(plane, SUB, (groups * full + 1) * LANES), (of_j * group_j, (full + 1) * LANES)],
+        [(plane, SUB, (groups * full + 1) * LANES), (of_j * group_j // 2, (full + 1) * LANES)],
         got,
     )
+    pairs = [(k, k ^ 1) for k in range(of_i)]
+    pair = lax.ppermute(text, "zm", pairs)
     image = exchange(mine, ("x", "y"))
-    part = call(functools.partial(logits_kernel, tiling), (plane * groups * SUB, of_j * group_j), image, text)
+    part = call(functools.partial(logits_kernel, tiling), (plane * groups * SUB, of_j * group_j), image, text, pair)
     other = lax.ppermute(part, "ze", [(0, 1), (1, 0)])
     both = lax.all_gather(part + other, "c")
-    grad_i, grad_t = call(
+    grad_i, grad_t, grad_pair = call(
         functools.partial(grads_kernel, (of_j, of_y, rows, group_i, group_j), tiling),
-        [image.shape, text.shape],
-        log_scale, logit_bias, both, image, text,
-        inputs=[SMEM] * 2 + [VMEM] * 3,
+        [image.shape, text.shape, text.shape],
+        log_scale, logit_bias, both, image, text, pair,
+        inputs=[SMEM] * 2 + [VMEM] * 4,
     )
+    back_t = lax.ppermute(grad_pair, "zm", pairs)
     back = exchange(grad_i, ("x", "y"))
-    sent = call(functools.partial(narrow_kernel, blocks, narrow), sent_shape, back, grad_t)
+    sent = call(functools.partial(narrow_kernel, blocks, narrow), sent_shape, back, grad_t, back_t)
     got = exchange(sent, ("zh", "zm"))
     out_i, out_t = call(functools.partial(collect_kernel, blocks), [(narrow, rows), (narrow, rows)], got)
     return (out_i.T, out_t.T)

time: 149 us -> 142 us (0.953)
  the two profiles are of different devices: /device:TPU:8 before, /device:TPU:20 now
where the time goes in v5:
time: 142 us; the launch traced here: 141 us
  blocking collectives  94.2 us (66%)
  starting transfers between devices  28.9 us (20%)
  waiting for transfers between devices  10.3 us (7%)
  Pallas kernels  5.91 us (4%)
  between operations  1.97 us (1%)
    all_to_all x2, blocking collectives, exchange(): return lax.all_to_all(value, axis, split_axis=0, concat_axis=0, tiled=True)  92 us
    all_to_all x2, starting transfers between devices, exchange(): return lax.all_to_all(value, axis, split_axis=0, concat_axis=0, tiled=True)  14.5 us
    pallas_call x6, Pallas kernels, call(): pl.pallas_call(kernel, out_shape=shapes if many else shapes[0], in_specs=...  5.91 us
    ppermute x1, starting transfers between devices, on_device(): pair = lax.ppermute(text, 'zm', pairs)  5.05 us
    ppermute x1, starting transfers between devices, on_device(): back_t = lax.ppermute(grad_pair, 'zm', pairs)  4.82 us
    ppermute x1, waiting for transfers between devices, on_device(): back_t = lax.ppermute(grad_pair, 'zm', pairs)  4.69 us
    ppermute x1, starting transfers between devices, on_device(): other = lax.ppermute(part, 'ze', [(0, 1), (1, 0)])  4.54 us
    ppermute x1, waiting for transfers between devices, on_device(): other = lax.ppermute(part, 'ze', [(0, 1), (1, 0)])  3.04 us
  transfers between devices with their start and end apart: 5, of which 3 were waited for; matrix products, arithmetic and copies ran while one was open for 0% of the time, Pallas kernels for 0%

profile of v5, /device:TPU:20, one launch (start us, length us, event | category | flops | bytes accessed | tf_op | source)
XLA Modules:
  0.0 141.3 jit_solution(8434803662897523735)
XLA Ops:
  0.6 0.9 shard_map.59
  1.6 54.2 %all_to_all.20.got_ref = f32[16,8,256]{2,1,0:T(8,128)S(1)} all-to-all(f32[16,8,256]{2,1,0:T(8,128)S(1)} %shard_map.59), channel_id=1, replica_groups=mesh['x'=4,'zh'=2,'y'=4,'zm'=8,'ze'=2,'c'=2] {'zh','zm'}, dimensions={0} | all-to-all | bytes 262144 | tf_op jit(solution)/shard_map/all_to_all | solution.py:241
  55.7 1.0 shard_map.60
  56.8 7.2 %all-to-all-start.1 = ((f32[16,8,1152]{2,1,0:T(8,128)}), f32[16,8,1152]{2,1,0:T(8,128)S(1)}, u32[]{:S(2)}, u32[]{:S(2)}) async-start(f32[16,8,1152]{2,1,0:T(8,128)} %get-tuple-element.9), calls=%async_computation.1 | async-start | bytes 1179648 | tf_op jit(solution)/shard_map/all_to_all | solution.py:241
  64.0 5.0 %collective-permute-start = (f32[64,384]{1,0:T(8,128)S(1)}, f32[64,384]{1,0:T(8,128)S(1)}, u32[]{:S(2)}, u32[]{:S(2)}) collective-permute-start(f32[64,384]{1,0:T(8,128)S(1)} %get-tuple-element.10.text_ref.refs_1_), channel_id=1, source_target_pairs={{0,4},{4,0},{8,12},{12,8},{16,20},{20,16},{24,28},{28,24},{1,5},{5... | collective-permute-start | bytes 294920 | tf_op jit(solution)/shard_map/ppermute | solution.py:270
  69.0 2.6 %collective-permute-done.pair_ref.refs_2_ = f32[64,384]{1,0:T(8,128)S(1)} collective-permute-done((f32[64,384]{1,0:T(8,128)S(1)}, f32[64,384]{1,0:T(8,128)S(1)}, u32[]{:S(2)}, u32[]{:S(2)}) %collective-permute-start) | collective-permute-done | bytes 98336 | tf_op jit(solution)/shard_map/ppermute | solution.py:270
  71.6 0.0 all-to-all-done.1.image_ref.refs_0_
  71.6 0.8 shard_map.61
  72.4 4.5 %collective-permute-start.1 = (f32[512,128]{1,0:T(8,128)S(1)}, f32[512,128]{1,0:T(8,128)S(1)}, u32[]{:S(2)}, u32[]{:S(2)}) collective-permute-start(f32[512,128]{1,0:T(8,128)S(1)} %shard_map.61), channel_id=1, source_target_pairs={{0,2},{2,0},{1,3},{3,1},{4,6},{6,4},{5,7},{7,5},{8,10},{10,8},{9,1... | collective-permute-start | bytes 786440 | tf_op jit(solution)/shard_map/ppermute | solution.py:273
  78.3 3.0 %collective-permute-done.1 = f32[512,128]{1,0:T(8,128)S(1)} collective-permute-done((f32[512,128]{1,0:T(8,128)S(1)}, f32[512,128]{1,0:T(8,128)S(1)}, u32[]{:S(2)}, u32[]{:S(2)}) %collective-permute-start.1) | collective-permute-done | bytes 262176 | tf_op jit(solution)/shard_map/ppermute | solution.py:273
  81.4 2.2 %all-gather = f32[1024,128]{1,0:T(8,128)S(1)} all-gather(f32[512,128]{1,0:T(8,128)S(1)} %add.3), channel_id=2, replica_groups=mesh['x'=4,'zh'=2,'y'=4,'zm'=8,'ze'=2,'c'=2] {'c'}, dimensions={0}, use_global_device_ids=true | all-gather | bytes 786432 | tf_op jit(solution)/shard_map/all_gather | solution.py:274
  83.5 2.1 %shard_map.62 = (f32[16,8,1152]{2,1,0:T(8,128)}, f32[64,384]{1,0:T(8,128)S(1)}, f32[64,384]{1,0:T(8,128)S(1)}) custom-call(f32[1]{0:T(128)S(6)} %copy.6.log_scale_ref, f32[1]{0:T(128)S(6)} %copy.7.bias_ref, f32[2,512,128]{2,1,0:T(8,128)S(1)} %bitcast.5, f32[16,8,1152]{2,1,0:T(8,128)S(1)} %all-to-all-done.1.image_ref.refs_0_, ...), custom_call_target="tpu_custom_call" | custom-call | tf_op jit(solution)/shard_map/pallas_call | solution.py:230
  85.6 7.2 %all-to-all-start.2 = ((f32[16,8,1152]{2,1,0:T(8,128)}), f32[16,8,1152]{2,1,0:T(8,128)S(1)}, u32[]{:S(2)}, u32[]{:S(2)}) async-start(f32[16,8,1152]{2,1,0:T(8,128)} %get-tuple-element.11), calls=%async_computation.2 | async-start | bytes 1179648 | tf_op jit(solution)/shard_map/all_to_all | solution.py:241
  92.8 4.8 %collective-permute-start.2 = (f32[64,384]{1,0:T(8,128)S(1)}, f32[64,384]{1,0:T(8,128)S(1)}, u32[]{:S(2)}, u32[]{:S(2)}) collective-permute-start(f32[64,384]{1,0:T(8,128)S(1)} %get-tuple-element.13), channel_id=1, source_target_pairs={{0,4},{4,0},{8,12},{12,8},{16,20},{20,16},{24,28},{28,24},{1,5},{5... | collective-permute-start | bytes 294920 | tf_op jit(solution)/shard_map/ppermute | solution.py:281
  97.7 4.7 %collective-permute-done.2.pair_ref = f32[64,384]{1,0:T(8,128)S(1)} collective-permute-done((f32[64,384]{1,0:T(8,128)S(1)}, f32[64,384]{1,0:T(8,128)S(1)}, u32[]{:S(2)}, u32[]{:S(2)}) %collective-permute-start.2) | collective-permute-done | bytes 98336 | tf_op jit(solution)/shard_map/ppermute | solution.py:281
  102.4 0.0 all-to-all-done.2.image_ref
  102.4 0.3 shard_map.63
  102.7 37.9 %all_to_all.21.got_ref = f32[16,8,256]{2,1,0:T(8,128)S(1)} all-to-all(f32[16,8,256]{2,1,0:T(8,128)S(1)} %shard_map.63), channel_id=1, replica_groups=mesh['x'=4,'zh'=2,'y'=4,'zm'=8,'ze'=2,'c'=2] {'zh','zm'}, dimensions={0} | all-to-all | bytes 262144 | tf_op jit(solution)/shard_map/all_to_all | solution.py:241
  140.6 0.8 shard_map.64
  (1 shorter events, 0.0 us)
Async XLA Ops:
  56.8 14.9 %all-to-all-start.1 = ((f32[16,8,1152]{2,1,0:T(8,128)}), f32[16,8,1152]{2,1,0:T(8,128)S(1)}, u32[]{:S(2)}, u32[]{:S(2)}) async-start(f32[16,8,1152]{2,1,0:T(8,128)} %get-tuple-element.9), calls=%async_computation.1 | async-start | bytes 1179648 | tf_op jit(solution)/shard_map/all_to_all | solution.py:241
  64.0 7.6 %collective-permute-start = (f32[64,384]{1,0:T(8,128)S(1)}, f32[64,384]{1,0:T(8,128)S(1)}, u32[]{:S(2)}, u32[]{:S(2)}) collective-permute-start(f32[64,384]{1,0:T(8,128)S(1)} %get-tuple-element.10.text_ref.refs_1_), channel_id=1, source_target_pairs={{0,4},{4,0},{8,12},{12,8},{16,20},{20,16},{24,28},{28,24},{1,5},{5... | collective-permute-start | bytes 294920 | tf_op jit(solution)/shard_map/ppermute | solution.py:270
  72.4 8.9 %collective-permute-start.1 = (f32[512,128]{1,0:T(8,128)S(1)}, f32[512,128]{1,0:T(8,128)S(1)}, u32[]{:S(2)}, u32[]{:S(2)}) collective-permute-start(f32[512,128]{1,0:T(8,128)S(1)} %shard_map.61), channel_id=1, source_target_pairs={{0,2},{2,0},{1,3},{3,1},{4,6},{6,4},{5,7},{7,5},{8,10},{10,8},{9,1... | collective-permute-start | bytes 786440 | tf_op jit(solution)/shard_map/ppermute | solution.py:273
  85.6 16.7 %all-to-all-start.2 = ((f32[16,8,1152]{2,1,0:T(8,128)}), f32[16,8,1152]{2,1,0:T(8,128)S(1)}, u32[]{:S(2)}, u32[]{:S(2)}) async-start(f32[16,8,1152]{2,1,0:T(8,128)} %get-tuple-element.11), calls=%async_computation.2 | async-start | bytes 1179648 | tf_op jit(solution)/shard_map/all_to_all | solution.py:241
  92.8 9.5 %collective-permute-start.2 = (f32[64,384]{1,0:T(8,128)S(1)}, f32[64,384]{1,0:T(8,128)S(1)}, u32[]{:S(2)}, u32[]{:S(2)}) collective-permute-start(f32[64,384]{1,0:T(8,128)S(1)} %get-tuple-element.13), channel_id=1, source_target_pairs={{0,4},{4,0},{8,12},{12,8},{16,20},{20,16},{24,28},{28,24},{1,5},{5... | collective-permute-start | bytes 294920 | tf_op jit(solution)/shard_map/ppermute | solution.py:281

commit v6 on v5

--- a/solution.py
+++ b/solution.py
@@ -87,11 +87,34 @@
                 out_ref[j * of_i + i, :, which * LANES : (which + 1) * LANES] = value
 
 
+def side_by_side(groups, full, rest):
+    found, shared, per = [], [], LANES // rest
+    for group, tiles in enumerate(groups):
+        found += [((group * full + which) * LANES, tiles[which]) for which in range(full)]
+        at = group % per * rest
+        moved = shift(tiles[full], at)
+        if at == 0:
+            shared.append(moved)
+        else:
+            shared[-1] = jnp.where(lanes_from(at, moved.shape), moved, shared[-1])
+    return found + [((len(groups) * full + k) * LANES, tile) for k, tile in enumerate(shared)]
+
+
+def apart(ref, groups, full, rest):
+    per = LANES // rest
+    found = []
+    for group in range(groups):
+        tiles = [ref[:, (group * full + k) * LANES : (group * full + k + 1) * LANES] for k in range(full)]
+        lo = (groups * full + group // per) * LANES
+        found.append(tiles + [shift(ref[:, lo : lo + LANES], -(group % per) * rest)])
+    return found
+
+
 def widen_kernel(sizes, narrow, got_ref, image_ref, text_ref):
     of_i, of_j, blocks_i, blocks_j = sizes
     copies = image_ref.shape[0]
     full, rest = divmod(of_i * narrow, LANES)
-    last = None
+    last, texts = None, []
     for j in range(of_j):
         sources = [reader(got_ref, j * of_i + i) for i in range(of_i)]
         for k in range(blocks_i + blocks_j):
@@ -105,10 +128,9 @@
                 moved = shift(tiles[full], group * rest)
                 last = moved if last is None else jnp.where(lanes_from(group * rest, moved.shape), moved, last)
             else:
-                at = (j * blocks_j + k - blocks_i) * SUB
-                tiles[full] = jnp.where(lanes_from(rest, tiles[full].shape), 0.0, tiles[full])
-                for which, value in enumerate(tiles):
-                    text_ref[at : at + SUB, which * LANES : (which + 1) * LANES] = value
+                texts.append(tiles)
+    for lane, value in side_by_side(texts, full, rest):
+        text_ref[:, lane : lane + LANES] = value
     lo = of_j * blocks_i * full * LANES
     for copy in range(copies):
         image_ref[copy, :, lo : lo + LANES] = last
@@ -131,16 +153,22 @@
 )
 
 
-def both_halves(text_ref, pair_ref):
-    return jnp.concatenate([text_ref[...], pair_ref[...]], axis=0)
-
-
-def logits_kernel(tiling, image_ref, text_ref, pair_ref, out_ref):
-    text = both_halves(text_ref, pair_ref)
+def both_halves(tiling, text_ref, pair_ref):
+    groups, full, rest = tiling
+    rows = []
+    for ref in (text_ref, pair_ref):
+        for tiles in apart(ref, groups, full, rest):
+            last = jnp.where(lanes_from(rest, tiles[full].shape), 0.0, tiles[full])
+            rows.append(jnp.concatenate(tiles[:full] + [last], axis=1))
+    return jnp.concatenate(rows, axis=0)
+
+
+def logits_kernel(tiling, text_tiling, image_ref, text_ref, pair_ref, out_ref):
+    text = both_halves(text_tiling, text_ref, pair_ref)
     out_ref[...] = dot(stacked(image_ref, *tiling), text, (((1,), (1,)), ((), ())))
 
 
-def grads_kernel(sizes, tiling, log_scale_ref, bias_ref, both_ref, *refs):
+def grads_kernel(sizes, tiling, text_tiling, log_scale_ref, bias_ref, both_ref, *refs):
     image_ref, text_ref, pair_ref, gi_ref, gt_ref, gt_pair_ref = refs
     high, of_y, rows, group_i, group_j = sizes
     groups, full, rest = tiling
@@ -154,14 +182,14 @@
     zh, inner = group // blocks_i, group % blocks_i * SUB + r % SUB
     row_ids = ((source // of_y * high + zh) * of_y + source % of_y) * rows + i * group_i + inner
     c = lax.broadcasted_iota(jnp.int32, logits.shape, 1)
-    half, of_half = group_j // 2, text_ref.shape[0]
+    half, of_half = group_j // 2, gt_ref.shape[0]
     which = (i + c // of_half) % 2
     zh, inner = c % of_half // half, c % half
     col_ids = ((x * high + zh) * of_y + y) * rows + j * group_j + which * half + inner
     label = jnp.where(row_ids == col_ids, 1.0, -1.0)
     coef = -label * jax.nn.sigmoid(-label * logits)
     coef = scale * coef
-    found = dot(coef, both_halves(text_ref, pair_ref), (((1,), (0,)), ((), ())))
+    found = dot(coef, both_halves(text_tiling, text_ref, pair_ref), (((1,), (0,)), ((), ())))
     last = None
     for group in range(groups):
         part = found[group * sources * SUB : (group + 1) * sources * SUB]
@@ -173,7 +201,10 @@
     gi_ref[:, :, lo : lo + LANES] = last.reshape(sources, SUB, LANES)
     found = dot(coef, stacked(image_ref, *tiling), (((0,), (0,)), ((), ())))
     gt_ref[...] = found[:of_half]
-    gt_pair_ref[...] = found[of_half:]
+    pair = [found[at : at + SUB] for at in range(of_half, 2 * of_half, SUB)]
+    pair = [[rows_of[:, k * LANES : (k + 1) * LANES] for k in range(full + 1)] for rows_of in pair]
+    for lane, value in side_by_side(pair, full, rest):
+        gt_pair_ref[:, lane : lane + LANES] = value
 
 
 def narrow_kernel(sizes, narrow, image_ref, text_ref, pair_ref, out_ref):
@@ -189,9 +220,11 @@
         row = tiles[group * full : (group + 1) * full] + [shift(tiles[lo], -group * rest)]
         return lambda which: row[which]
 
+    pair = apart(pair_ref, of_j * blocks_j, full, rest)
+
     def text_row(start):
-        own, pair = reader(text_ref, None, start), reader(pair_ref, None, start)
-        row = [own(which) + pair(which) for which in range(full + 1)]
+        own = reader(text_ref, None, start)
+        row = [own(which) + pair[start // SUB][which] for which in range(full + 1)]
         return lambda which: row[which]
 
     for j in range(of_j):
@@ -251,6 +284,10 @@
     assert 0 < rest * groups <= LANES
     tiling = (groups, full, rest)
     plane = of_x * of_y
+    text_groups = of_j * blocks[3]
+    text_tiling = (text_groups, full, rest)
+    text_shape = (SUB, (text_groups * full + -(-text_groups // (LANES // rest))) * LANES)
+    grad_shape = (text_groups * SUB, (full + 1) * LANES)
     sent_shape = (of_j * of_i, SUB, tiles_of((blocks[2] + blocks[3]) * narrow) * LANES)
     block = pltpu.VMEM((narrow, rows), jnp.float32)
 
@@ -263,18 +300,18 @@
     got = exchange(sent, ("zh", "zm"))
     mine, text = call(
         functools.partial(widen_kernel, blocks, narrow),
-        [(plane, SUB, (groups * full + 1) * LANES), (of_j * group_j // 2, (full + 1) * LANES)],
+        [(plane, SUB, (groups * full + 1) * LANES), text_shape],
         got,
     )
     pairs = [(k, k ^ 1) for k in range(of_i)]
     pair = lax.ppermute(text, "zm", pairs)
     image = exchange(mine, ("x", "y"))
-    part = call(functools.partial(logits_kernel, tiling), (plane * groups * SUB, of_j * group_j), image, text, pair)
+    part = call(functools.partial(logits_kernel, tiling, text_tiling), (plane * groups * SUB, of_j * group_j), image, text, pair)
     other = lax.ppermute(part, "ze", [(0, 1), (1, 0)])
     both = lax.all_gather(part + other, "c")
     grad_i, grad_t, grad_pair = call(
-        functools.partial(grads_kernel, (of_j, of_y, rows, group_i, group_j), tiling),
-        [image.shape, text.shape, text.shape],
+        functools.partial(grads_kernel, (of_j, of_y, rows, group_i, group_j), tiling, text_tiling),
+        [image.shape, grad_shape, text_shape],
         log_scale, logit_bias, both, image, text, pair,
         inputs=[SMEM] * 2 + [VMEM] * 4,
     )

time: 142 us -> 141 us (level)
  the two profiles are of different devices: /device:TPU:20 before, /device:TPU:8 now
where the time goes in v6:
time: 141 us; the launch traced here: 140 us
  blocking collectives  91.5 us (65%)
  starting transfers between devices  26.2 us (19%)
  waiting for transfers between devices  14.5 us (10%)
  Pallas kernels  6.16 us (4%)
  between operations  1.98 us (1%)
    all_to_all x2, blocking collectives, exchange(): return lax.all_to_all(value, axis, split_axis=0, concat_axis=0, tiled=True)  89.3 us
    all_to_all x2, starting transfers between devices, exchange(): return lax.all_to_all(value, axis, split_axis=0, concat_axis=0, tiled=True)  13.5 us
    pallas_call x6, Pallas kernels, call(): pl.pallas_call(kernel, out_shape=shapes if many else shapes[0], in_specs=...  6.16 us
    ppermute x1, starting transfers between devices, on_device(): pair = lax.ppermute(text, 'zm', pairs)  5.05 us
    ppermute x1, starting transfers between devices, on_device(): back_t = lax.ppermute(grad_pair, 'zm', pairs)  4.8 us
    ppermute x1, waiting for transfers between devices, on_device(): other = lax.ppermute(part, 'ze', [(0, 1), (1, 0)])  4.13 us
    all_to_all x2, waiting for transfers between devices, exchange(): return lax.all_to_all(value, axis, split_axis=0, concat_axis=0, tiled=True)  4.13 us
    ppermute x1, waiting for transfers between devices, on_device(): back_t = lax.ppermute(grad_pair, 'zm', pairs)  3.91 us
  transfers between devices with their start and end apart: 5, of which 5 were waited for; matrix products, arithmetic and copies ran while one was open for 0% of the time, Pallas kernels for 0%

profile of v6, /device:TPU:8, one launch (start us, length us, event | category | flops | bytes accessed | tf_op | source)
XLA Modules:
  0.0 140.3 jit_solution(9633039236809660356)
XLA Ops:
  0.6 0.9 shard_map.59
  1.6 54.2 %all_to_all.20.got_ref = f32[16,8,256]{2,1,0:T(8,128)S(1)} all-to-all(f32[16,8,256]{2,1,0:T(8,128)S(1)} %shard_map.59), channel_id=1, replica_groups=mesh['x'=4,'zh'=2,'y'=4,'zm'=8,'ze'=2,'c'=2] {'zh','zm'}, dimensions={0} | all-to-all | bytes 262144 | tf_op jit(solution)/shard_map/all_to_all | solution.py:274
  55.7 1.1 shard_map.60
  56.8 7.4 %all-to-all-start.1 = ((f32[16,8,1152]{2,1,0:T(8,128)}), f32[16,8,1152]{2,1,0:T(8,128)S(1)}, u32[]{:S(2)}, u32[]{:S(2)}) async-start(f32[16,8,1152]{2,1,0:T(8,128)} %get-tuple-element.9), calls=%async_computation.1 | async-start | bytes 1179648 | tf_op jit(solution)/shard_map/all_to_all | solution.py:274
  64.2 5.0 %collective-permute-start = (f32[8,2304]{1,0:T(8,128)S(1)}, f32[8,2304]{1,0:T(8,128)S(1)}, u32[]{:S(2)}, u32[]{:S(2)}) collective-permute-start(f32[8,2304]{1,0:T(8,128)S(1)} %get-tuple-element.10.text_ref.refs_1_), channel_id=1, source_target_pairs={{0,4},{4,0},{8,12},{12,8},{16,20},{20,16},{24,28},{28,24},{1,5},{5... | collective-permute-start | bytes 221192 | tf_op jit(solution)/shard_map/ppermute | solution.py:307
  69.2 2.3 %collective-permute-done.pair_ref.refs_2_ = f32[8,2304]{1,0:T(8,128)S(1)} collective-permute-done((f32[8,2304]{1,0:T(8,128)S(1)}, f32[8,2304]{1,0:T(8,128)S(1)}, u32[]{:S(2)}, u32[]{:S(2)}) %collective-permute-start) | collective-permute-done | bytes 73760 | tf_op jit(solution)/shard_map/ppermute | solution.py:307
  71.6 1.7 %all-to-all-done.1.image_ref.refs_0_ = f32[16,8,1152]{2,1,0:T(8,128)S(1)} async-done(((f32[16,8,1152]{2,1,0:T(8,128)}), f32[16,8,1152]{2,1,0:T(8,128)S(1)}, u32[]{:S(2)}, u32[]{:S(2)}) %all-to-all-start.1) | async-done | bytes 589856 | tf_op jit(solution)/shard_map/all_to_all | solution.py:274
  73.3 0.8 shard_map.61
  74.1 2.8 %collective-permute-start.1 = (f32[512,128]{1,0:T(8,128)S(1)}, f32[512,128]{1,0:T(8,128)S(1)}, u32[]{:S(2)}, u32[]{:S(2)}) collective-permute-start(f32[512,128]{1,0:T(8,128)S(1)} %shard_map.61), channel_id=1, source_target_pairs={{0,2},{2,0},{1,3},{3,1},{4,6},{6,4},{5,7},{7,5},{8,10},{10,8},{9,1... | collective-permute-start | bytes 786440 | tf_op jit(solution)/shard_map/ppermute | solution.py:310
  78.2 4.1 %collective-permute-done.1 = f32[512,128]{1,0:T(8,128)S(1)} collective-permute-done((f32[512,128]{1,0:T(8,128)S(1)}, f32[512,128]{1,0:T(8,128)S(1)}, u32[]{:S(2)}, u32[]{:S(2)}) %collective-permute-start.1) | collective-permute-done | bytes 262176 | tf_op jit(solution)/shard_map/ppermute | solution.py:310
  82.4 2.2 %all-gather = f32[1024,128]{1,0:T(8,128)S(1)} all-gather(f32[512,128]{1,0:T(8,128)S(1)} %add.3), channel_id=2, replica_groups=mesh['x'=4,'zh'=2,'y'=4,'zm'=8,'ze'=2,'c'=2] {'c'}, dimensions={0}, use_global_device_ids=true | all-gather | bytes 786432 | tf_op jit(solution)/shard_map/all_gather | solution.py:311
  84.6 2.3 %shard_map.62 = (f32[16,8,1152]{2,1,0:T(8,128)}, f32[64,384]{1,0:T(8,128)S(1)}, f32[8,2304]{1,0:T(8,128)S(1)}) custom-call(f32[1]{0:T(128)S(6)} %copy.6.log_scale_ref, f32[1]{0:T(128)S(6)} %copy.7.bias_ref, f32[2,512,128]{2,1,0:T(8,128)S(1)} %bitcast.5, f32[16,8,1152]{2,1,0:T(8,128)S(1)} %all-to-all-done.1.image_ref.refs_0_, ...), custom_call_target="tpu_custom_call" | custom-call | tf_op jit(solution)/shard_map/pallas_call | solution.py:263
  86.9 6.1 %all-to-all-start.2 = ((f32[16,8,1152]{2,1,0:T(8,128)}), f32[16,8,1152]{2,1,0:T(8,128)S(1)}, u32[]{:S(2)}, u32[]{:S(2)}) async-start(f32[16,8,1152]{2,1,0:T(8,128)} %get-tuple-element.11), calls=%async_computation.2 | async-start | bytes 1179648 | tf_op jit(solution)/shard_map/all_to_all | solution.py:274
  93.0 4.8 %collective-permute-start.2 = (f32[8,2304]{1,0:T(8,128)S(1)}, f32[8,2304]{1,0:T(8,128)S(1)}, u32[]{:S(2)}, u32[]{:S(2)}) collective-permute-start(f32[8,2304]{1,0:T(8,128)S(1)} %get-tuple-element.13), channel_id=1, source_target_pairs={{0,4},{4,0},{8,12},{12,8},{16,20},{20,16},{24,28},{28,24},{1,5},{5... | collective-permute-start | bytes 221192 | tf_op jit(solution)/shard_map/ppermute | solution.py:318
  97.8 3.9 %collective-permute-done.2.pair_ref = f32[8,2304]{1,0:T(8,128)S(1)} collective-permute-done((f32[8,2304]{1,0:T(8,128)S(1)}, f32[8,2304]{1,0:T(8,128)S(1)}, u32[]{:S(2)}, u32[]{:S(2)}) %collective-permute-start.2) | collective-permute-done | bytes 73760 | tf_op jit(solution)/shard_map/ppermute | solution.py:318
  101.7 2.4 %all-to-all-done.2.image_ref = f32[16,8,1152]{2,1,0:T(8,128)S(1)} async-done(((f32[16,8,1152]{2,1,0:T(8,128)}), f32[16,8,1152]{2,1,0:T(8,128)S(1)}, u32[]{:S(2)}, u32[]{:S(2)}) %all-to-all-start.2) | async-done | bytes 589856 | tf_op jit(solution)/shard_map/all_to_all | solution.py:274
  104.1 0.3 shard_map.63
  104.4 35.1 %all_to_all.21.got_ref = f32[16,8,256]{2,1,0:T(8,128)S(1)} all-to-all(f32[16,8,256]{2,1,0:T(8,128)S(1)} %shard_map.63), channel_id=1, replica_groups=mesh['x'=4,'zh'=2,'y'=4,'zm'=8,'ze'=2,'c'=2] {'zh','zm'}, dimensions={0} | all-to-all | bytes 262144 | tf_op jit(solution)/shard_map/all_to_all | solution.py:274
  139.6 0.8 shard_map.64
  (1 shorter events, 0.0 us)
Async XLA Ops:
  56.8 16.5 %all-to-all-start.1 = ((f32[16,8,1152]{2,1,0:T(8,128)}), f32[16,8,1152]{2,1,0:T(8,128)S(1)}, u32[]{:S(2)}, u32[]{:S(2)}) async-start(f32[16,8,1152]{2,1,0:T(8,128)} %get-tuple-element.9), calls=%async_computation.1 | async-start | bytes 1179648 | tf_op jit(solution)/shard_map/all_to_all | solution.py:274
  64.2 7.4 %collective-permute-start = (f32[8,2304]{1,0:T(8,128)S(1)}, f32[8,2304]{1,0:T(8,128)S(1)}, u32[]{:S(2)}, u32[]{:S(2)}) collective-permute-start(f32[8,2304]{1,0:T(8,128)S(1)} %get-tuple-element.10.text_ref.refs_1_), channel_id=1, source_target_pairs={{0,4},{4,0},{8,12},{12,8},{16,20},{20,16},{24,28},{28,24},{1,5},{5... | collective-permute-start | bytes 221192 | tf_op jit(solution)/shard_map/ppermute | solution.py:307
  74.1 8.3 %collective-permute-start.1 = (f32[512,128]{1,0:T(8,128)S(1)}, f32[512,128]{1,0:T(8,128)S(1)}, u32[]{:S(2)}, u32[]{:S(2)}) collective-permute-start(f32[512,128]{1,0:T(8,128)S(1)} %shard_map.61), channel_id=1, source_target_pairs={{0,2},{2,0},{1,3},{3,1},{4,6},{6,4},{5,7},{7,5},{8,10},{10,8},{9,1... | collective-permute-start | bytes 786440 | tf_op jit(solution)/shard_map/ppermute | solution.py:310
  86.9 17.3 %all-to-all-start.2 = ((f32[16,8,1152]{2,1,0:T(8,128)}), f32[16,8,1152]{2,1,0:T(8,128)S(1)}, u32[]{:S(2)}, u32[]{:S(2)}) async-start(f32[16,8,1152]{2,1,0:T(8,128)} %get-tuple-element.11), calls=%async_computation.2 | async-start | bytes 1179648 | tf_op jit(solution)/shard_map/all_to_all | solution.py:274
  93.0 8.7 %collective-permute-start.2 = (f32[8,2304]{1,0:T(8,128)S(1)}, f32[8,2304]{1,0:T(8,128)S(1)}, u32[]{:S(2)}, u32[]{:S(2)}) collective-permute-start(f32[8,2304]{1,0:T(8,128)S(1)} %get-tuple-element.13), channel_id=1, source_target_pairs={{0,4},{4,0},{8,12},{12,8},{16,20},{20,16},{24,28},{28,24},{1,5},{5... | collective-permute-start | bytes 221192 | tf_op jit(solution)/shard_map/ppermute | solution.py:318

commit v7 on v6

--- a/solution.py
+++ b/solution.py
@@ -163,18 +163,21 @@
     return jnp.concatenate(rows, axis=0)
 
 
-def logits_kernel(tiling, text_tiling, image_ref, text_ref, pair_ref, out_ref):
+def logits_kernel(tiling, text_tiling, image_ref, text_ref, pair_ref, *out_refs):
     text = both_halves(text_tiling, text_ref, pair_ref)
-    out_ref[...] = dot(stacked(image_ref, *tiling), text, (((1,), (1,)), ((), ())))
-
-
-def grads_kernel(sizes, tiling, text_tiling, log_scale_ref, bias_ref, both_ref, *refs):
-    image_ref, text_ref, pair_ref, gi_ref, gt_ref, gt_pair_ref = refs
+    found = dot(stacked(image_ref, *tiling), text, (((1,), (1,)), ((), ())))
+    rows = out_refs[0].shape[0]
+    for k, out_ref in enumerate(out_refs):
+        out_ref[...] = found[k * rows : (k + 1) * rows]
+
+
+def image_grads_kernel(sizes, tiling, text_tiling, log_scale_ref, bias_ref, first_ref, second_ref, text_ref, pair_ref, gi_ref, coef_ref):
     high, of_y, rows, group_i, group_j = sizes
     groups, full, rest = tiling
-    sources = image_ref.shape[0]
+    sources = gi_ref.shape[0]
     scale = jnp.exp(jnp.full((1, 1), log_scale_ref[0], jnp.float32))
-    logits = scale * (both_ref[0] + both_ref[1]) + bias_ref[0]
+    summed = jnp.concatenate([ref[0] + ref[1] for ref in (first_ref, second_ref)], axis=0)
+    logits = scale * summed + bias_ref[0]
     x, y, i, j = (lax.axis_index(a) for a in ("x", "y", "zm", "zh"))
     r = lax.broadcasted_iota(jnp.int32, logits.shape, 0)
     group, source = r // (sources * SUB), r % (sources * SUB) // SUB
@@ -182,13 +185,14 @@
     zh, inner = group // blocks_i, group % blocks_i * SUB + r % SUB
     row_ids = ((source // of_y * high + zh) * of_y + source % of_y) * rows + i * group_i + inner
     c = lax.broadcasted_iota(jnp.int32, logits.shape, 1)
-    half, of_half = group_j // 2, gt_ref.shape[0]
+    half, of_half = group_j // 2, logits.shape[1] // 2
     which = (i + c // of_half) % 2
     zh, inner = c % of_half // half, c % half
     col_ids = ((x * high + zh) * of_y + y) * rows + j * group_j + which * half + inner
     label = jnp.where(row_ids == col_ids, 1.0, -1.0)
     coef = -label * jax.nn.sigmoid(-label * logits)
     coef = scale * coef
+    coef_ref[...] = coef
     found = dot(coef, both_halves(text_tiling, text_ref, pair_ref), (((1,), (0,)), ((), ())))
     last = None
     for group in range(groups):
@@ -199,7 +203,12 @@
         last = moved if last is None else last + moved
     lo = groups * full * LANES
     gi_ref[:, :, lo : lo + LANES] = last.reshape(sources, SUB, LANES)
-    found = dot(coef, stacked(image_ref, *tiling), (((0,), (0,)), ((), ())))
+
+
+def text_grads_kernel(tiling, coef_ref, image_ref, gt_ref, gt_pair_ref):
+    _, full, rest = tiling
+    of_half = gt_ref.shape[0]
+    found = dot(coef_ref[...], stacked(image_ref, *tiling), (((0,), (0,)), ((), ())))
     gt_ref[...] = found[:of_half]
     pair = [found[at : at + SUB] for at in range(of_half, 2 * of_half, SUB)]
     pair = [[rows_of[:, k * LANES : (k + 1) * LANES] for k in range(full + 1)] for rows_of in pair]
@@ -306,15 +315,19 @@
     pairs = [(k, k ^ 1) for k in range(of_i)]
     pair = lax.ppermute(text, "zm", pairs)
     image = exchange(mine, ("x", "y"))
-    part = call(functools.partial(logits_kernel, tiling, text_tiling), (plane * groups * SUB, of_j * group_j), image, text, pair)
-    other = lax.ppermute(part, "ze", [(0, 1), (1, 0)])
-    both = lax.all_gather(part + other, "c")
-    grad_i, grad_t, grad_pair = call(
-        functools.partial(grads_kernel, (of_j, of_y, rows, group_i, group_j), tiling, text_tiling),
-        [image.shape, grad_shape, text_shape],
-        log_scale, logit_bias, both, image, text, pair,
+    shape = (plane * groups * SUB, of_j * group_j)
+    parts = call(
+        functools.partial(logits_kernel, tiling, text_tiling), [(shape[0] // 2, shape[1])] * 2, image, text, pair
+    )
+    others = [lax.ppermute(part, "ze", [(0, 1), (1, 0)]) for part in parts]
+    both = [lax.all_gather(part + other, "c") for part, other in zip(parts, others)]
+    grad_i, coef = call(
+        functools.partial(image_grads_kernel, (of_j, of_y, rows, group_i, group_j), tiling, text_tiling),
+        [image.shape, shape],
+        log_scale, logit_bias, *both, text, pair,
         inputs=[SMEM] * 2 + [VMEM] * 4,
     )
+    grad_t, grad_pair = call(functools.partial(text_grads_kernel, tiling), [grad_shape, text_shape], coef, image)
     back_t = lax.ppermute(grad_pair, "zm", pairs)
     back = exchange(grad_i, ("x", "y"))
     sent = call(functools.partial(narrow_kernel, blocks, narrow), sent_shape, back, grad_t, back_t)

time: 141 us -> 142 us (level)
  waiting for transfers between devices: 14.5 us -> 10.2 us
  starting transfers between devices: 26.2 us -> 30.3 us
    ppermute x1 -> x2, waiting for transfers between devices: 4.13 us -> 0.54 us  [on_device(): others = [lax.ppermute(part, 'ze', [(0, 1), (1, 0)]) for part in parts]]
    ppermute x1 -> x2, starting transfers between devices: 2.83 us -> 5.84 us  [on_device(): others = [lax.ppermute(part, 'ze', [(0, 1), (1, 0)]) for part in parts]]
    all_gather x1 -> x2, blocking collectives: 2.18 us -> 3.99 us  [on_device(): lax.all_gather(part + other, 'c')]
    pallas_call x6 -> x7, Pallas kernels: 6.16 us -> 6.48 us  [call(): pl.pallas_call(kernel, out_shape=shapes if many else shapes[0], in_specs=...]
  transfers between devices with their start and end apart: 5 -> 6, of which waited for: 5 -> 5; matrix products, arithmetic and copies ran while one was open for 0% -> 0% of each run, Pallas kernels for 0% -> 1%
where the time goes in v7:
time: 142 us; the launch traced here: 141 us
  blocking collectives  92 us (65%)
  starting transfers between devices  30.3 us (21%)
  waiting for transfers between devices  10.2 us (7%)
  Pallas kernels  6.48 us (5%)
  between operations  1.99 us (1%)
    all_to_all x2, blocking collectives, exchange(): return lax.all_to_all(value, axis, split_axis=0, concat_axis=0, tiled=True)  88 us
    all_to_all x2, starting transfers between devices, exchange(): return lax.all_to_all(value, axis, split_axis=0, concat_axis=0, tiled=True)  14.6 us
    pallas_call x7, Pallas kernels, call(): pl.pallas_call(kernel, out_shape=shapes if many else shapes[0], in_specs=...  6.48 us
    ppermute x2, starting transfers between devices, on_device(): others = [lax.ppermute(part, 'ze', [(0, 1), (1, 0)]) for part in parts]  5.84 us
    ppermute x1, starting transfers between devices, on_device(): pair = lax.ppermute(text, 'zm', pairs)  5.05 us
    ppermute x1, starting transfers between devices, on_device(): back_t = lax.ppermute(grad_pair, 'zm', pairs)  4.81 us
    all_gather x2, blocking collectives, on_device(): lax.all_gather(part + other, 'c')  3.99 us
    all_to_all x2, waiting for transfers between devices, exchange(): return lax.all_to_all(value, axis, split_axis=0, concat_axis=0, tiled=True)  3.87 us
  transfers between devices with their start and end apart: 6, of which 5 were waited for; matrix products, arithmetic and copies ran while one was open for 0% of the time, Pallas kernels for 1%

profile of v7, /device:TPU:8, one launch (start us, length us, event | category | flops | bytes accessed | tf_op | source)
XLA Modules:
  0.0 140.9 jit_solution(1240139641397935369)
XLA Ops:
  0.6 0.9 shard_map.59
  1.6 54.2 %all_to_all.20.got_ref = f32[16,8,256]{2,1,0:T(8,128)S(1)} all-to-all(f32[16,8,256]{2,1,0:T(8,128)S(1)} %shard_map.59), channel_id=1, replica_groups=mesh['x'=4,'zh'=2,'y'=4,'zm'=8,'ze'=2,'c'=2] {'zh','zm'}, dimensions={0} | all-to-all | bytes 262144 | tf_op jit(solution)/shard_map/all_to_all | solution.py:283
  55.7 1.1 shard_map.60
  56.8 7.4 %all-to-all-start.1 = ((f32[16,8,1152]{2,1,0:T(8,128)}), f32[16,8,1152]{2,1,0:T(8,128)S(1)}, u32[]{:S(2)}, u32[]{:S(2)}) async-start(f32[16,8,1152]{2,1,0:T(8,128)} %get-tuple-element.12), calls=%async_computation.1 | async-start | bytes 1179648 | tf_op jit(solution)/shard_map/all_to_all | solution.py:283
  64.2 5.0 %collective-permute-start = (f32[8,2304]{1,0:T(8,128)S(1)}, f32[8,2304]{1,0:T(8,128)S(1)}, u32[]{:S(2)}, u32[]{:S(2)}) collective-permute-start(f32[8,2304]{1,0:T(8,128)S(1)} %get-tuple-element.13.text_ref), channel_id=1, source_target_pairs={{0,4},{4,0},{8,12},{12,8},{16,20},{20,16},{24,28},{28,24},{1,5},{5... | collective-permute-start | bytes 221192 | tf_op jit(solution)/shard_map/ppermute | solution.py:316
  69.2 2.3 %collective-permute-done.pair_ref = f32[8,2304]{1,0:T(8,128)S(1)} collective-permute-done((f32[8,2304]{1,0:T(8,128)S(1)}, f32[8,2304]{1,0:T(8,128)S(1)}, u32[]{:S(2)}, u32[]{:S(2)}) %collective-permute-start) | collective-permute-done | bytes 73760 | tf_op jit(solution)/shard_map/ppermute | solution.py:316
  71.6 1.7 %all-to-all-done.1.image_ref = f32[16,8,1152]{2,1,0:T(8,128)S(1)} async-done(((f32[16,8,1152]{2,1,0:T(8,128)}), f32[16,8,1152]{2,1,0:T(8,128)S(1)}, u32[]{:S(2)}, u32[]{:S(2)}) %all-to-all-start.1) | async-done | bytes 589856 | tf_op jit(solution)/shard_map/all_to_all | solution.py:283
  73.3 0.8 shard_map.61
  74.1 2.8 %collective-permute-start.1 = (f32[256,128]{1,0:T(8,128)S(1)}, f32[256,128]{1,0:T(8,128)S(1)}, u32[]{:S(2)}, u32[]{:S(2)}) collective-permute-start(f32[256,128]{1,0:T(8,128)S(1)} %get-tuple-element.14), channel_id=1, source_target_pairs={{0,2},{2,0},{1,3},{3,1},{4,6},{6,4},{5,7},{7,5},{8,10},{10,8},{9,1... | collective-permute-start | bytes 393224 | tf_op jit(solution)/shard_map/ppermute | solution.py:322
  76.9 3.0 %collective-permute-start.2 = (f32[256,128]{1,0:T(8,128)S(1)}, f32[256,128]{1,0:T(8,128)S(1)}, u32[]{:S(2)}, u32[]{:S(2)}) collective-permute-start(f32[256,128]{1,0:T(8,128)S(1)} %get-tuple-element.15), channel_id=1, source_target_pairs={{0,2},{2,0},{1,3},{3,1},{4,6},{6,4},{5,7},{7,5},{8,10},{10,8},{9,1... | collective-permute-start | bytes 393224 | tf_op jit(solution)/shard_map/ppermute | solution.py:322
  81.2 0.0 collective-permute-done.1
  81.3 2.0 %all-gather = f32[512,128]{1,0:T(8,128)S(1)} all-gather(f32[256,128]{1,0:T(8,128)S(1)} %add.6), channel_id=2, replica_groups=mesh['x'=4,'zh'=2,'y'=4,'zm'=8,'ze'=2,'c'=2] {'c'}, dimensions={0}, use_global_device_ids=true | all-gather | bytes 393216 | tf_op jit(solution)/shard_map/all_gather | solution.py:323
  83.3 0.5 collective-permute-done.2
  83.8 2.0 %all-gather.1 = f32[512,128]{1,0:T(8,128)S(1)} all-gather(f32[256,128]{1,0:T(8,128)S(1)} %add.7), channel_id=3, replica_groups=mesh['x'=4,'zh'=2,'y'=4,'zm'=8,'ze'=2,'c'=2] {'c'}, dimensions={0}, use_global_device_ids=true | all-gather | bytes 393216 | tf_op jit(solution)/shard_map/all_gather | solution.py:323
  85.8 1.9 %shard_map.62 = (f32[16,8,1152]{2,1,0:T(8,128)}, f32[512,128]{1,0:T(8,128)S(1)}) custom-call(f32[1]{0:T(128)S(6)} %copy.6.log_scale_ref, f32[1]{0:T(128)S(6)} %copy.7.bias_ref, f32[2,256,128]{2,1,0:T(8,128)S(1)} %bitcast.6, f32[2,256,128]{2,1,0:T(8,128)S(1)} %bitcast.7, f32[8,2304]{1,0:T(8,128)S(1)} %get-tuple-element.13.text_ref, ...), custom_call_target="tpu_custom_call" | custom-call | tf_op jit(solution)/shard_map/pallas_call | solution.py:272
  87.7 7.2 %all-to-all-start.2 = ((f32[16,8,1152]{2,1,0:T(8,128)}), f32[16,8,1152]{2,1,0:T(8,128)S(1)}, u32[]{:S(2)}, u32[]{:S(2)}) async-start(f32[16,8,1152]{2,1,0:T(8,128)} %get-tuple-element.16), calls=%async_computation.2 | async-start | bytes 1179648 | tf_op jit(solution)/shard_map/all_to_all | solution.py:283
  94.9 0.7 shard_map.63
  95.7 4.8 %collective-permute-start.3 = (f32[8,2304]{1,0:T(8,128)S(1)}, f32[8,2304]{1,0:T(8,128)S(1)}, u32[]{:S(2)}, u32[]{:S(2)}) collective-permute-start(f32[8,2304]{1,0:T(8,128)S(1)} %get-tuple-element.19), channel_id=1, source_target_pairs={{0,4},{4,0},{8,12},{12,8},{16,20},{20,16},{24,28},{28,24},{1,5},{5... | collective-permute-start | bytes 221192 | tf_op jit(solution)/shard_map/ppermute | solution.py:331
  100.5 3.4 %collective-permute-done.3.pair_ref = f32[8,2304]{1,0:T(8,128)S(1)} collective-permute-done((f32[8,2304]{1,0:T(8,128)S(1)}, f32[8,2304]{1,0:T(8,128)S(1)}, u32[]{:S(2)}, u32[]{:S(2)}) %collective-permute-start.3) | collective-permute-done | bytes 73760 | tf_op jit(solution)/shard_map/ppermute | solution.py:331
  103.9 2.2 %all-to-all-done.2.image_ref = f32[16,8,1152]{2,1,0:T(8,128)S(1)} async-done(((f32[16,8,1152]{2,1,0:T(8,128)}), f32[16,8,1152]{2,1,0:T(8,128)S(1)}, u32[]{:S(2)}, u32[]{:S(2)}) %all-to-all-start.2) | async-done | bytes 589856 | tf_op jit(solution)/shard_map/all_to_all | solution.py:283
  106.1 0.3 shard_map.64
  106.4 33.8 %all_to_all.21.got_ref = f32[16,8,256]{2,1,0:T(8,128)S(1)} all-to-all(f32[16,8,256]{2,1,0:T(8,128)S(1)} %shard_map.64), channel_id=1, replica_groups=mesh['x'=4,'zh'=2,'y'=4,'zm'=8,'ze'=2,'c'=2] {'zh','zm'}, dimensions={0} | all-to-all | bytes 262144 | tf_op jit(solution)/shard_map/all_to_all | solution.py:283
  140.2 0.8 shard_map.65
  (2 shorter events, 0.0 us)
Async XLA Ops:
  56.8 16.5 %all-to-all-start.1 = ((f32[16,8,1152]{2,1,0:T(8,128)}), f32[16,8,1152]{2,1,0:T(8,128)S(1)}, u32[]{:S(2)}, u32[]{:S(2)}) async-start(f32[16,8,1152]{2,1,0:T(8,128)} %get-tuple-element.12), calls=%async_computation.1 | async-start | bytes 1179648 | tf_op jit(solution)/shard_map/all_to_all | solution.py:283
  64.2 7.4 %collective-permute-start = (f32[8,2304]{1,0:T(8,128)S(1)}, f32[8,2304]{1,0:T(8,128)S(1)}, u32[]{:S(2)}, u32[]{:S(2)}) collective-permute-start(f32[8,2304]{1,0:T(8,128)S(1)} %get-tuple-element.13.text_ref), channel_id=1, source_target_pairs={{0,4},{4,0},{8,12},{12,8},{16,20},{20,16},{24,28},{28,24},{1,5},{5... | collective-permute-start | bytes 221192 | tf_op jit(solution)/shard_map/ppermute | solution.py:316
  74.1 7.2 %collective-permute-start.1 = (f32[256,128]{1,0:T(8,128)S(1)}, f32[256,128]{1,0:T(8,128)S(1)}, u32[]{:S(2)}, u32[]{:S(2)}) collective-permute-start(f32[256,128]{1,0:T(8,128)S(1)} %get-tuple-element.14), channel_id=1, source_target_pairs={{0,2},{2,0},{1,3},{3,1},{4,6},{6,4},{5,7},{7,5},{8,10},{10,8},{9,1... | collective-permute-start | bytes 393224 | tf_op jit(solution)/shard_map/ppermute | solution.py:322
  76.9 6.9 %collective-permute-start.2 = (f32[256,128]{1,0:T(8,128)S(1)}, f32[256,128]{1,0:T(8,128)S(1)}, u32[]{:S(2)}, u32[]{:S(2)}) collective-permute-start(f32[256,128]{1,0:T(8,128)S(1)} %get-tuple-element.15), channel_id=1, source_target_pairs={{0,2},{2,0},{1,3},{3,1},{4,6},{6,4},{5,7},{7,5},{8,10},{10,8},{9,1... | collective-permute-start | bytes 393224 | tf_op jit(solution)/shard_map/ppermute | solution.py:322
  87.7 18.4 %all-to-all-start.2 = ((f32[16,8,1152]{2,1,0:T(8,128)}), f32[16,8,1152]{2,1,0:T(8,128)S(1)}, u32[]{:S(2)}, u32[]{:S(2)}) async-start(f32[16,8,1152]{2,1,0:T(8,128)} %get-tuple-element.16), calls=%async_computation.2 | async-start | bytes 1179648 | tf_op jit(solution)/shard_map/all_to_all | solution.py:283
  95.7 8.2 %collective-permute-start.3 = (f32[8,2304]{1,0:T(8,128)S(1)}, f32[8,2304]{1,0:T(8,128)S(1)}, u32[]{:S(2)}, u32[]{:S(2)}) collective-permute-start(f32[8,2304]{1,0:T(8,128)S(1)} %get-tuple-element.19), channel_id=1, source_target_pairs={{0,4},{4,0},{8,12},{12,8},{16,20},{20,16},{24,28},{28,24},{1,5},{5... | collective-permute-start | bytes 221192 | tf_op jit(solution)/shard_map/ppermute | solution.py:331

commit v8 on v7

--- a/solution.py
+++ b/solution.py
@@ -163,21 +163,21 @@
     return jnp.concatenate(rows, axis=0)
 
 
-def logits_kernel(tiling, text_tiling, image_ref, text_ref, pair_ref, *out_refs):
+def logits_kernel(tiling, text_tiling, log_scale_ref, bias_ref, image_ref, text_ref, pair_ref, *out_refs):
     text = both_halves(text_tiling, text_ref, pair_ref)
-    found = dot(stacked(image_ref, *tiling), text, (((1,), (1,)), ((), ())))
+    scale = jnp.exp(jnp.full((1, 1), log_scale_ref[0], jnp.float32))
+    found = scale * dot(stacked(image_ref, *tiling), text, (((1,), (1,)), ((), ()))) + 0.25 * bias_ref[0]
     rows = out_refs[0].shape[0]
     for k, out_ref in enumerate(out_refs):
         out_ref[...] = found[k * rows : (k + 1) * rows]
 
 
-def image_grads_kernel(sizes, tiling, text_tiling, log_scale_ref, bias_ref, first_ref, second_ref, text_ref, pair_ref, gi_ref, coef_ref):
+def image_grads_kernel(sizes, tiling, text_tiling, log_scale_ref, first_ref, second_ref, text_ref, pair_ref, gi_ref, coef_ref):
     high, of_y, rows, group_i, group_j = sizes
     groups, full, rest = tiling
     sources = gi_ref.shape[0]
     scale = jnp.exp(jnp.full((1, 1), log_scale_ref[0], jnp.float32))
-    summed = jnp.concatenate([ref[0] + ref[1] for ref in (first_ref, second_ref)], axis=0)
-    logits = scale * summed + bias_ref[0]
+    logits = jnp.concatenate([ref[0] + ref[1] for ref in (first_ref, second_ref)], axis=0)
     x, y, i, j = (lax.axis_index(a) for a in ("x", "y", "zm", "zh"))
     r = lax.broadcasted_iota(jnp.int32, logits.shape, 0)
     group, source = r // (sources * SUB), r % (sources * SUB) // SUB
@@ -317,15 +317,16 @@
     image = exchange(mine, ("x", "y"))
     shape = (plane * groups * SUB, of_j * group_j)
     parts = call(
-        functools.partial(logits_kernel, tiling, text_tiling), [(shape[0] // 2, shape[1])] * 2, image, text, pair
+        functools.partial(logits_kernel, tiling, text_tiling), [(shape[0] // 2, shape[1])] * 2,
+        log_scale, logit_bias, image, text, pair, inputs=[SMEM] * 2 + [VMEM] * 3,
     )
     others = [lax.ppermute(part, "ze", [(0, 1), (1, 0)]) for part in parts]
     both = [lax.all_gather(part + other, "c") for part, other in zip(parts, others)]
     grad_i, coef = call(
         functools.partial(image_grads_kernel, (of_j, of_y, rows, group_i, group_j), tiling, text_tiling),
         [image.shape, shape],
-        log_scale, logit_bias, *both, text, pair,
-        inputs=[SMEM] * 2 + [VMEM] * 4,
+        log_scale, *both, text, pair,
+        inputs=[SMEM] + [VMEM] * 4,
     )
     grad_t, grad_pair = call(functools.partial(text_grads_kernel, tiling), [grad_shape, text_shape], coef, image)
     back_t = lax.ppermute(grad_pair, "zm", pairs)

time: 142 us -> 142 us (level)
  transfers between devices with their start and end apart: 6 -> 6, of which waited for: 5 -> 6; matrix products, arithmetic and copies ran while one was open for 0% -> 0% of each run, Pallas kernels for 1% -> 1%
where the time goes in v8:
time: 142 us; the launch traced here: 141 us
  blocking collectives  92 us (65%)
  starting transfers between devices  30.3 us (21%)
  waiting for transfers between devices  10.2 us (7%)
  Pallas kernels  6.47 us (5%)
  between operations  1.98 us (1%)
    all_to_all x2, blocking collectives, exchange(): return lax.all_to_all(value, axis, split_axis=0, concat_axis=0, tiled=True)  88 us
    all_to_all x2, starting transfers between devices, exchange(): return lax.all_to_all(value, axis, split_axis=0, concat_axis=0, tiled=True)  14.6 us
    pallas_call x7, Pallas kernels, call(): pl.pallas_call(kernel, out_shape=shapes if many else shapes[0], in_specs=...  6.47 us
    ppermute x2, starting transfers between devices, on_device(): others = [lax.ppermute(part, 'ze', [(0, 1), (1, 0)]) for part in parts]  5.84 us
    ppermute x1, starting transfers between devices, on_device(): pair = lax.ppermute(text, 'zm', pairs)  5.05 us
    ppermute x1, starting transfers between devices, on_device(): back_t = lax.ppermute(grad_pair, 'zm', pairs)  4.81 us
    all_to_all x2, waiting for transfers between devices, exchange(): return lax.all_to_all(value, axis, split_axis=0, concat_axis=0, tiled=True)  4.18 us
    all_gather x2, blocking collectives, on_device(): lax.all_gather(part + other, 'c')  3.99 us
  transfers between devices with their start and end apart: 6, of which 6 were waited for; matrix products, arithmetic and copies ran while one was open for 0% of the time, Pallas kernels for 1%

profile of v8, /device:TPU:8, one launch (start us, length us, event | category | flops | bytes accessed | tf_op | source)
XLA Modules:
  0.0 140.9 jit_solution(7912358352198058572)
XLA Ops:
  0.6 0.9 shard_map.59
  1.6 54.2 %all_to_all.20.got_ref = f32[16,8,256]{2,1,0:T(8,128)S(1)} all-to-all(f32[16,8,256]{2,1,0:T(8,128)S(1)} %shard_map.59), channel_id=1, replica_groups=mesh['x'=4,'zh'=2,'y'=4,'zm'=8,'ze'=2,'c'=2] {'zh','zm'}, dimensions={0} | all-to-all | bytes 262144 | tf_op jit(solution)/shard_map/all_to_all | solution.py:283
  55.7 1.1 shard_map.60
  56.8 7.4 %all-to-all-start.1 = ((f32[16,8,1152]{2,1,0:T(8,128)}), f32[16,8,1152]{2,1,0:T(8,128)S(1)}, u32[]{:S(2)}, u32[]{:S(2)}) async-start(f32[16,8,1152]{2,1,0:T(8,128)} %get-tuple-element.12), calls=%async_computation.1 | async-start | bytes 1179648 | tf_op jit(solution)/shard_map/all_to_all | solution.py:283
  64.2 5.0 %collective-permute-start = (f32[8,2304]{1,0:T(8,128)S(1)}, f32[8,2304]{1,0:T(8,128)S(1)}, u32[]{:S(2)}, u32[]{:S(2)}) collective-permute-start(f32[8,2304]{1,0:T(8,128)S(1)} %get-tuple-element.13.text_ref), channel_id=1, source_target_pairs={{0,4},{4,0},{8,12},{12,8},{16,20},{20,16},{24,28},{28,24},{1,5},{5... | collective-permute-start | bytes 221192 | tf_op jit(solution)/shard_map/ppermute | solution.py:316
  70.5 1.0 collective-permute-done.pair_ref
  71.6 1.7 %all-to-all-done.1.image_ref = f32[16,8,1152]{2,1,0:T(8,128)S(1)} async-done(((f32[16,8,1152]{2,1,0:T(8,128)}), f32[16,8,1152]{2,1,0:T(8,128)S(1)}, u32[]{:S(2)}, u32[]{:S(2)}) %all-to-all-start.1) | async-done | bytes 589856 | tf_op jit(solution)/shard_map/all_to_all | solution.py:283
  73.3 0.8 shard_map.61
  74.1 2.8 %collective-permute-start.1 = (f32[256,128]{1,0:T(8,128)S(1)}, f32[256,128]{1,0:T(8,128)S(1)}, u32[]{:S(2)}, u32[]{:S(2)}) collective-permute-start(f32[256,128]{1,0:T(8,128)S(1)} %get-tuple-element.14), channel_id=1, source_target_pairs={{0,2},{2,0},{1,3},{3,1},{4,6},{6,4},{5,7},{7,5},{8,10},{10,8},{9,1... | collective-permute-start | bytes 393224 | tf_op jit(solution)/shard_map/ppermute | solution.py:323
  76.9 3.0 %collective-permute-start.2 = (f32[256,128]{1,0:T(8,128)S(1)}, f32[256,128]{1,0:T(8,128)S(1)}, u32[]{:S(2)}, u32[]{:S(2)}) collective-permute-start(f32[256,128]{1,0:T(8,128)S(1)} %get-tuple-element.15), channel_id=1, source_target_pairs={{0,2},{2,0},{1,3},{3,1},{4,6},{6,4},{5,7},{7,5},{8,10},{10,8},{9,1... | collective-permute-start | bytes 393224 | tf_op jit(solution)/shard_map/ppermute | solution.py:323
  79.9 1.0 collective-permute-done.1
  81.0 2.0 %all-gather = f32[512,128]{1,0:T(8,128)S(1)} all-gather(f32[256,128]{1,0:T(8,128)S(1)} %add.6), channel_id=2, replica_groups=mesh['x'=4,'zh'=2,'y'=4,'zm'=8,'ze'=2,'c'=2] {'c'}, dimensions={0}, use_global_device_ids=true | all-gather | bytes 393216 | tf_op jit(solution)/shard_map/all_gather | solution.py:324
  83.0 0.8 collective-permute-done.2
  83.8 2.0 %all-gather.1 = f32[512,128]{1,0:T(8,128)S(1)} all-gather(f32[256,128]{1,0:T(8,128)S(1)} %add.7), channel_id=3, replica_groups=mesh['x'=4,'zh'=2,'y'=4,'zm'=8,'ze'=2,'c'=2] {'c'}, dimensions={0}, use_global_device_ids=true | all-gather | bytes 393216 | tf_op jit(solution)/shard_map/all_gather | solution.py:324
  85.8 1.9 %shard_map.62 = (f32[16,8,1152]{2,1,0:T(8,128)}, f32[512,128]{1,0:T(8,128)S(1)}) custom-call(f32[1]{0:T(128)S(6)} %copy.6.log_scale_ref, f32[2,256,128]{2,1,0:T(8,128)S(1)} %bitcast.6, f32[2,256,128]{2,1,0:T(8,128)S(1)} %bitcast.7, f32[8,2304]{1,0:T(8,128)S(1)} %get-tuple-element.13.text_ref, f32[8,2304]{1,0:T(8,128)S(1)} %collective-permute-done.pair_ref), custom_call_target="tpu_custom_call" | custom-call | tf_op jit(solution)/shard_map/pallas_call | solution.py:272
  87.7 7.2 %all-to-all-start.2 = ((f32[16,8,1152]{2,1,0:T(8,128)}), f32[16,8,1152]{2,1,0:T(8,128)S(1)}, u32[]{:S(2)}, u32[]{:S(2)}) async-start(f32[16,8,1152]{2,1,0:T(8,128)} %get-tuple-element.16), calls=%async_computation.2 | async-start | bytes 1179648 | tf_op jit(solution)/shard_map/all_to_all | solution.py:283
  94.9 0.7 shard_map.63
  95.7 4.8 %collective-permute-start.3 = (f32[8,2304]{1,0:T(8,128)S(1)}, f32[8,2304]{1,0:T(8,128)S(1)}, u32[]{:S(2)}, u32[]{:S(2)}) collective-permute-start(f32[8,2304]{1,0:T(8,128)S(1)} %get-tuple-element.19), channel_id=1, source_target_pairs={{0,4},{4,0},{8,12},{12,8},{16,20},{20,16},{24,28},{28,24},{1,5},{5... | collective-permute-start | bytes 221192 | tf_op jit(solution)/shard_map/ppermute | solution.py:332
  100.5 3.1 %collective-permute-done.3.pair_ref = f32[8,2304]{1,0:T(8,128)S(1)} collective-permute-done((f32[8,2304]{1,0:T(8,128)S(1)}, f32[8,2304]{1,0:T(8,128)S(1)}, u32[]{:S(2)}, u32[]{:S(2)}) %collective-permute-start.3) | collective-permute-done | bytes 73760 | tf_op jit(solution)/shard_map/ppermute | solution.py:332
  103.6 2.5 %all-to-all-done.2.image_ref = f32[16,8,1152]{2,1,0:T(8,128)S(1)} async-done(((f32[16,8,1152]{2,1,0:T(8,128)}), f32[16,8,1152]{2,1,0:T(8,128)S(1)}, u32[]{:S(2)}, u32[]{:S(2)}) %all-to-all-start.2) | async-done | bytes 589856 | tf_op jit(solution)/shard_map/all_to_all | solution.py:283
  106.1 0.3 shard_map.64
  106.4 33.8 %all_to_all.21.got_ref = f32[16,8,256]{2,1,0:T(8,128)S(1)} all-to-all(f32[16,8,256]{2,1,0:T(8,128)S(1)} %shard_map.64), channel_id=1, replica_groups=mesh['x'=4,'zh'=2,'y'=4,'zm'=8,'ze'=2,'c'=2] {'zh','zm'}, dimensions={0} | all-to-all | bytes 262144 | tf_op jit(solution)/shard_map/all_to_all | solution.py:283
  140.2 0.8 shard_map.65
  (2 shorter events, 0.0 us)
Async XLA Ops:
  56.8 16.5 %all-to-all-start.1 = ((f32[16,8,1152]{2,1,0:T(8,128)}), f32[16,8,1152]{2,1,0:T(8,128)S(1)}, u32[]{:S(2)}, u32[]{:S(2)}) async-start(f32[16,8,1152]{2,1,0:T(8,128)} %get-tuple-element.12), calls=%async_computation.1 | async-start | bytes 1179648 | tf_op jit(solution)/shard_map/all_to_all | solution.py:283
  64.2 7.4 %collective-permute-start = (f32[8,2304]{1,0:T(8,128)S(1)}, f32[8,2304]{1,0:T(8,128)S(1)}, u32[]{:S(2)}, u32[]{:S(2)}) collective-permute-start(f32[8,2304]{1,0:T(8,128)S(1)} %get-tuple-element.13.text_ref), channel_id=1, source_target_pairs={{0,4},{4,0},{8,12},{12,8},{16,20},{20,16},{24,28},{28,24},{1,5},{5... | collective-permute-start | bytes 221192 | tf_op jit(solution)/shard_map/ppermute | solution.py:316
  74.1 6.9 %collective-permute-start.1 = (f32[256,128]{1,0:T(8,128)S(1)}, f32[256,128]{1,0:T(8,128)S(1)}, u32[]{:S(2)}, u32[]{:S(2)}) collective-permute-start(f32[256,128]{1,0:T(8,128)S(1)} %get-tuple-element.14), channel_id=1, source_target_pairs={{0,2},{2,0},{1,3},{3,1},{4,6},{6,4},{5,7},{7,5},{8,10},{10,8},{9,1... | collective-permute-start | bytes 393224 | tf_op jit(solution)/shard_map/ppermute | solution.py:323
  76.9 6.9 %collective-permute-start.2 = (f32[256,128]{1,0:T(8,128)S(1)}, f32[256,128]{1,0:T(8,128)S(1)}, u32[]{:S(2)}, u32[]{:S(2)}) collective-permute-start(f32[256,128]{1,0:T(8,128)S(1)} %get-tuple-element.15), channel_id=1, source_target_pairs={{0,2},{2,0},{1,3},{3,1},{4,6},{6,4},{5,7},{7,5},{8,10},{10,8},{9,1... | collective-permute-start | bytes 393224 | tf_op jit(solution)/shard_map/ppermute | solution.py:323
  87.7 18.4 %all-to-all-start.2 = ((f32[16,8,1152]{2,1,0:T(8,128)}), f32[16,8,1152]{2,1,0:T(8,128)S(1)}, u32[]{:S(2)}, u32[]{:S(2)}) async-start(f32[16,8,1152]{2,1,0:T(8,128)} %get-tuple-element.16), calls=%async_computation.2 | async-start | bytes 1179648 | tf_op jit(solution)/shard_map/all_to_all | solution.py:283
  95.7 7.9 %collective-permute-start.3 = (f32[8,2304]{1,0:T(8,128)S(1)}, f32[8,2304]{1,0:T(8,128)S(1)}, u32[]{:S(2)}, u32[]{:S(2)}) collective-permute-start(f32[8,2304]{1,0:T(8,128)S(1)} %get-tuple-element.19), channel_id=1, source_target_pairs={{0,4},{4,0},{8,12},{12,8},{16,20},{20,16},{24,28},{28,24},{1,5},{5... | collective-permute-start | bytes 221192 | tf_op jit(solution)/shard_map/ppermute | solution.py:332

commit v9 on v6

--- a/solution.py
+++ b/solution.py
@@ -168,11 +168,10 @@
     out_ref[...] = dot(stacked(image_ref, *tiling), text, (((1,), (1,)), ((), ())))
 
 
-def grads_kernel(sizes, tiling, text_tiling, log_scale_ref, bias_ref, both_ref, *refs):
-    image_ref, text_ref, pair_ref, gi_ref, gt_ref, gt_pair_ref = refs
+def image_grads_kernel(sizes, tiling, text_tiling, log_scale_ref, bias_ref, both_ref, text_ref, pair_ref, gi_ref, coef_ref):
     high, of_y, rows, group_i, group_j = sizes
     groups, full, rest = tiling
-    sources = image_ref.shape[0]
+    sources = gi_ref.shape[0]
     scale = jnp.exp(jnp.full((1, 1), log_scale_ref[0], jnp.float32))
     logits = scale * (both_ref[0] + both_ref[1]) + bias_ref[0]
     x, y, i, j = (lax.axis_index(a) for a in ("x", "y", "zm", "zh"))
@@ -182,13 +181,14 @@
     zh, inner = group // blocks_i, group % blocks_i * SUB + r % SUB
     row_ids = ((source // of_y * high + zh) * of_y + source % of_y) * rows + i * group_i + inner
     c = lax.broadcasted_iota(jnp.int32, logits.shape, 1)
-    half, of_half = group_j // 2, gt_ref.shape[0]
+    half, of_half = group_j // 2, logits.shape[1] // 2
     which = (i + c // of_half) % 2
     zh, inner = c % of_half // half, c % half
     col_ids = ((x * high + zh) * of_y + y) * rows + j * group_j + which * half + inner
     label = jnp.where(row_ids == col_ids, 1.0, -1.0)
     coef = -label * jax.nn.sigmoid(-label * logits)
     coef = scale * coef
+    coef_ref[...] = coef
     found = dot(coef, both_halves(text_tiling, text_ref, pair_ref), (((1,), (0,)), ((), ())))
     last = None
     for group in range(groups):
@@ -199,7 +199,12 @@
         last = moved if last is None else last + moved
     lo = groups * full * LANES
     gi_ref[:, :, lo : lo + LANES] = last.reshape(sources, SUB, LANES)
-    found = dot(coef, stacked(image_ref, *tiling), (((0,), (0,)), ((), ())))
+
+
+def text_grads_kernel(tiling, coef_ref, image_ref, gt_ref, gt_pair_ref):
+    _, full, rest = tiling
+    of_half = gt_ref.shape[0]
+    found = dot(coef_ref[...], stacked(image_ref, *tiling), (((0,), (0,)), ((), ())))
     gt_ref[...] = found[:of_half]
     pair = [found[at : at + SUB] for at in range(of_half, 2 * of_half, SUB)]
     pair = [[rows_of[:, k * LANES : (k + 1) * LANES] for k in range(full + 1)] for rows_of in pair]
@@ -309,12 +314,13 @@
     part = call(functools.partial(logits_kernel, tiling, text_tiling), (plane * groups * SUB, of_j * group_j), image, text, pair)
     other = lax.ppermute(part, "ze", [(0, 1), (1, 0)])
     both = lax.all_gather(part + other, "c")
-    grad_i, grad_t, grad_pair = call(
-        functools.partial(grads_kernel, (of_j, of_y, rows, group_i, group_j), tiling, text_tiling),
-        [image.shape, grad_shape, text_shape],
-        log_scale, logit_bias, both, image, text, pair,
-        inputs=[SMEM] * 2 + [VMEM] * 4,
+    grad_i, coef = call(
+        functools.partial(image_grads_kernel, (of_j, of_y, rows, group_i, group_j), tiling, text_tiling),
+        [image.shape, part.shape],
+        log_scale, logit_bias, both, text, pair,
+        inputs=[SMEM] * 2 + [VMEM] * 3,
     )
+    grad_t, grad_pair = call(functools.partial(text_grads_kernel, tiling), [grad_shape, text_shape], coef, image)
     back_t = lax.ppermute(grad_pair, "zm", pairs)
     back = exchange(grad_i, ("x", "y"))
     sent = call(functools.partial(narrow_kernel, blocks, narrow), sent_shape, back, grad_t, back_t)

time: 141 us -> 141 us (level)
  the two profiles are of different devices: /device:TPU:8 before, /device:TPU:22 now
where the time goes in v9:
time: 141 us; the launch traced here: 140 us
  blocking collectives  93.5 us (66%)
  starting transfers between devices  28.8 us (20%)
  waiting for transfers between devices  9.26 us (7%)
  Pallas kernels  6.46 us (5%)
  between operations  1.98 us (1%)
    all_to_all x2, blocking collectives, exchange(): return lax.all_to_all(value, axis, split_axis=0, concat_axis=0, tiled=True)  91.4 us
    all_to_all x2, starting transfers between devices, exchange(): return lax.all_to_all(value, axis, split_axis=0, concat_axis=0, tiled=True)  14.4 us
    pallas_call x7, Pallas kernels, call(): pl.pallas_call(kernel, out_shape=shapes if many else shapes[0], in_specs=...  6.46 us
    ppermute x1, starting transfers between devices, on_device(): pair = lax.ppermute(text, 'zm', pairs)  5.05 us
    ppermute x1, starting transfers between devices, on_device(): back_t = lax.ppermute(grad_pair, 'zm', pairs)  4.82 us
    ppermute x1, starting transfers between devices, on_device(): other = lax.ppermute(part, 'ze', [(0, 1), (1, 0)])  4.56 us
    ppermute x1, waiting for transfers between devices, on_device(): back_t = lax.ppermute(grad_pair, 'zm', pairs)  3.9 us
    ppermute x1, waiting for transfers between devices, on_device(): other = lax.ppermute(part, 'ze', [(0, 1), (1, 0)])  3.04 us
  transfers between devices with their start and end apart: 5, of which 3 were waited for; matrix products, arithmetic and copies ran while one was open for 0% of the time, Pallas kernels for 1%

profile of v9, /device:TPU:22, one launch (start us, length us, event | category | flops | bytes accessed | tf_op | source)
XLA Modules:
  0.0 140.1 jit_solution(8672783428109649221)
XLA Ops:
  0.6 0.9 shard_map.59
  1.6 54.2 %all_to_all.20.got_ref = f32[16,8,256]{2,1,0:T(8,128)S(1)} all-to-all(f32[16,8,256]{2,1,0:T(8,128)S(1)} %shard_map.59), channel_id=1, replica_groups=mesh['x'=4,'zh'=2,'y'=4,'zm'=8,'ze'=2,'c'=2] {'zh','zm'}, dimensions={0} | all-to-all | bytes 262144 | tf_op jit(solution)/shard_map/all_to_all | solution.py:279
  55.7 1.1 shard_map.60
  56.8 7.2 %all-to-all-start.1 = ((f32[16,8,1152]{2,1,0:T(8,128)}), f32[16,8,1152]{2,1,0:T(8,128)S(1)}, u32[]{:S(2)}, u32[]{:S(2)}) async-start(f32[16,8,1152]{2,1,0:T(8,128)} %get-tuple-element.10), calls=%async_computation.1 | async-start | bytes 1179648 | tf_op jit(solution)/shard_map/all_to_all | solution.py:279
  64.0 5.0 %collective-permute-start = (f32[8,2304]{1,0:T(8,128)S(1)}, f32[8,2304]{1,0:T(8,128)S(1)}, u32[]{:S(2)}, u32[]{:S(2)}) collective-permute-start(f32[8,2304]{1,0:T(8,128)S(1)} %get-tuple-element.11.text_ref), channel_id=1, source_target_pairs={{0,4},{4,0},{8,12},{12,8},{16,20},{20,16},{24,28},{28,24},{1,5},{5... | collective-permute-start | bytes 221192 | tf_op jit(solution)/shard_map/ppermute | solution.py:312
  69.0 2.3 %collective-permute-done.pair_ref = f32[8,2304]{1,0:T(8,128)S(1)} collective-permute-done((f32[8,2304]{1,0:T(8,128)S(1)}, f32[8,2304]{1,0:T(8,128)S(1)}, u32[]{:S(2)}, u32[]{:S(2)}) %collective-permute-start) | collective-permute-done | bytes 73760 | tf_op jit(solution)/shard_map/ppermute | solution.py:312
  71.4 0.0 all-to-all-done.1.image_ref
  71.4 0.8 shard_map.61
  72.2 4.6 %collective-permute-start.1 = (f32[512,128]{1,0:T(8,128)S(1)}, f32[512,128]{1,0:T(8,128)S(1)}, u32[]{:S(2)}, u32[]{:S(2)}) collective-permute-start(f32[512,128]{1,0:T(8,128)S(1)} %shard_map.61), channel_id=1, source_target_pairs={{0,2},{2,0},{1,3},{3,1},{4,6},{6,4},{5,7},{7,5},{8,10},{10,8},{9,1... | collective-permute-start | bytes 786440 | tf_op jit(solution)/shard_map/ppermute | solution.py:315
  78.0 3.0 %collective-permute-done.1 = f32[512,128]{1,0:T(8,128)S(1)} collective-permute-done((f32[512,128]{1,0:T(8,128)S(1)}, f32[512,128]{1,0:T(8,128)S(1)}, u32[]{:S(2)}, u32[]{:S(2)}) %collective-permute-start.1) | collective-permute-done | bytes 262176 | tf_op jit(solution)/shard_map/ppermute | solution.py:315
  81.1 2.2 %all-gather = f32[1024,128]{1,0:T(8,128)S(1)} all-gather(f32[512,128]{1,0:T(8,128)S(1)} %add.3), channel_id=2, replica_groups=mesh['x'=4,'zh'=2,'y'=4,'zm'=8,'ze'=2,'c'=2] {'c'}, dimensions={0}, use_global_device_ids=true | all-gather | bytes 786432 | tf_op jit(solution)/shard_map/all_gather | solution.py:316
  83.3 1.9 %shard_map.62 = (f32[16,8,1152]{2,1,0:T(8,128)}, f32[512,128]{1,0:T(8,128)S(1)}) custom-call(f32[1]{0:T(128)S(6)} %copy.6.log_scale_ref, f32[1]{0:T(128)S(6)} %copy.7.bias_ref, f32[2,512,128]{2,1,0:T(8,128)S(1)} %bitcast.5, f32[8,2304]{1,0:T(8,128)S(1)} %get-tuple-element.11.text_ref, f32[8,2304]{1,0:T(8,128)S(1)} %collective-permute-done.pair_ref), custom_call_target="tpu_custom_call" | custom-call | tf_op jit(solution)/shard_map/pallas_call | solution.py:268
  85.2 7.2 %all-to-all-start.2 = ((f32[16,8,1152]{2,1,0:T(8,128)}), f32[16,8,1152]{2,1,0:T(8,128)S(1)}, u32[]{:S(2)}, u32[]{:S(2)}) async-start(f32[16,8,1152]{2,1,0:T(8,128)} %get-tuple-element.12), calls=%async_computation.2 | async-start | bytes 1179648 | tf_op jit(solution)/shard_map/all_to_all | solution.py:279
  92.4 0.7 shard_map.63
  93.1 4.8 %collective-permute-start.2 = (f32[8,2304]{1,0:T(8,128)S(1)}, f32[8,2304]{1,0:T(8,128)S(1)}, u32[]{:S(2)}, u32[]{:S(2)}) collective-permute-start(f32[8,2304]{1,0:T(8,128)S(1)} %get-tuple-element.15), channel_id=1, source_target_pairs={{0,4},{4,0},{8,12},{12,8},{16,20},{20,16},{24,28},{28,24},{1,5},{5... | collective-permute-start | bytes 221192 | tf_op jit(solution)/shard_map/ppermute | solution.py:324
  97.9 3.9 %collective-permute-done.2.pair_ref = f32[8,2304]{1,0:T(8,128)S(1)} collective-permute-done((f32[8,2304]{1,0:T(8,128)S(1)}, f32[8,2304]{1,0:T(8,128)S(1)}, u32[]{:S(2)}, u32[]{:S(2)}) %collective-permute-start.2) | collective-permute-done | bytes 73760 | tf_op jit(solution)/shard_map/ppermute | solution.py:324
  101.8 0.0 all-to-all-done.2.image_ref
  101.8 0.3 shard_map.64
  102.1 37.2 %all_to_all.21.got_ref = f32[16,8,256]{2,1,0:T(8,128)S(1)} all-to-all(f32[16,8,256]{2,1,0:T(8,128)S(1)} %shard_map.64), channel_id=1, replica_groups=mesh['x'=4,'zh'=2,'y'=4,'zm'=8,'ze'=2,'c'=2] {'zh','zm'}, dimensions={0} | all-to-all | bytes 262144 | tf_op jit(solution)/shard_map/all_to_all | solution.py:279
  139.4 0.8 shard_map.65
  (1 shorter events, 0.0 us)
Async XLA Ops:
  56.8 14.6 %all-to-all-start.1 = ((f32[16,8,1152]{2,1,0:T(8,128)}), f32[16,8,1152]{2,1,0:T(8,128)S(1)}, u32[]{:S(2)}, u32[]{:S(2)}) async-start(f32[16,8,1152]{2,1,0:T(8,128)} %get-tuple-element.10), calls=%async_computation.1 | async-start | bytes 1179648 | tf_op jit(solution)/shard_map/all_to_all | solution.py:279
  64.0 7.4 %collective-permute-start = (f32[8,2304]{1,0:T(8,128)S(1)}, f32[8,2304]{1,0:T(8,128)S(1)}, u32[]{:S(2)}, u32[]{:S(2)}) collective-permute-start(f32[8,2304]{1,0:T(8,128)S(1)} %get-tuple-element.11.text_ref), channel_id=1, source_target_pairs={{0,4},{4,0},{8,12},{12,8},{16,20},{20,16},{24,28},{28,24},{1,5},{5... | collective-permute-start | bytes 221192 | tf_op jit(solution)/shard_map/ppermute | solution.py:312
  72.2 8.9 %collective-permute-start.1 = (f32[512,128]{1,0:T(8,128)S(1)}, f32[512,128]{1,0:T(8,128)S(1)}, u32[]{:S(2)}, u32[]{:S(2)}) collective-permute-start(f32[512,128]{1,0:T(8,128)S(1)} %shard_map.61), channel_id=1, source_target_pairs={{0,2},{2,0},{1,3},{3,1},{4,6},{6,4},{5,7},{7,5},{8,10},{10,8},{9,1... | collective-permute-start | bytes 786440 | tf_op jit(solution)/shard_map/ppermute | solution.py:315
  85.2 16.7 %all-to-all-start.2 = ((f32[16,8,1152]{2,1,0:T(8,128)}), f32[16,8,1152]{2,1,0:T(8,128)S(1)}, u32[]{:S(2)}, u32[]{:S(2)}) async-start(f32[16,8,1152]{2,1,0:T(8,128)} %get-tuple-element.12), calls=%async_computation.2 | async-start | bytes 1179648 | tf_op jit(solution)/shard_map/all_to_all | solution.py:279
  93.1 8.7 %collective-permute-start.2 = (f32[8,2304]{1,0:T(8,128)S(1)}, f32[8,2304]{1,0:T(8,128)S(1)}, u32[]{:S(2)}, u32[]{:S(2)}) collective-permute-start(f32[8,2304]{1,0:T(8,128)S(1)} %get-tuple-element.15), channel_id=1, source_target_pairs={{0,4},{4,0},{8,12},{12,8},{16,20},{20,16},{24,28},{28,24},{1,5},{5... | collective-permute-start | bytes 221192 | tf_op jit(solution)/shard_map/ppermute | solution.py:324
